TPU v7x, 512 devices: a whole 4x4x16 slice. The times are simulated.
512 devices in a mesh: gx: 64 (over x, z_lo, core), gy: 8 (over y, z_hi).
Axes of the slice: x: 4, y: 4, z: 16 (z_hi: 2, z_lo: 8; z = z_hi * 8 + z_lo), core: 2. Of those that a mesh axis runs over, the one named last changes fastest.
Arguments:
- normals: float32 [1, 2, 4096, 4096], P(None, None, 'gx', 'gy'), may hold values from -6 to 6
- plane_length: float32 [2], replicated, may hold values from 2 to 32
- plane_amplitude: float32 [2], replicated, may hold values from 0.4 to 1.4
- plane_mean: float32 [2], replicated, may hold values from -1 to 1
Outputs:
- coarse_log: float32 [1, 1, 2048, 2048], P(None, None, 'gx', 'gy')
All inputs are finite; a program needn't handle non-finite values.
Results may differ from a plain program's by a relative error of at most 0.000088.
Values sent between devices are 32-bit elements; how exact they have to be, the bound alone decides.
No kernel may reach another device: no remote copies, remote signals or barrier semaphores. Data moves between devices by JAX's collectives and lax.ppermute only.
A program may use at most 64 MiB of HBM per device.

v0:
```python
import math

import jax
import jax.numpy as jnp
from jax import lax
from jax.sharding import PartitionSpec as P

exactness = lax.Precision.HIGHEST


def first_tables(outer_len):
    row_ids = jnp.arange(outer_len, dtype=jnp.int32)[:, None]
    col_ids = jnp.arange(2 * outer_len, dtype=jnp.int32)[None, :]
    phase_index = row_ids * (2 * col_ids + 1) % (4 * outer_len)
    phases = phase_index.astype(jnp.float32) * (math.pi / (2 * outer_len))
    return (jnp.cos(phases), jnp.sin(phases))


def second_tables(inner_len, outer_len):
    total_len = inner_len * outer_len
    row_ids = jnp.arange(inner_len, dtype=jnp.int32)[:, None, None]
    high_ids = jnp.arange(inner_len // 2, dtype=jnp.int32)[None, :, None]
    low_ids = jnp.arange(2 * outer_len, dtype=jnp.int32)[None, None, :]
    position = high_ids * (2 * outer_len) + low_ids
    phase_index = row_ids * (2 * position + 1) % (4 * total_len)
    phases = phase_index.astype(jnp.float32) * (math.pi / (2 * total_len))
    return (jnp.cos(phases), jnp.sin(phases))


def cosine_weights(start, amount, total_len):
    wave_ids = (start + jnp.arange(amount, dtype=jnp.int32)).astype(jnp.float32)
    weight = jnp.where(wave_ids == 0, jnp.sqrt(1.0 / total_len), jnp.sqrt(2.0 / total_len))
    return (wave_ids, weight.astype(jnp.float32))


def harmonic_log(values):
    items, planes, first_len, second_len = values.shape
    blocks = jnp.exp(-values).reshape(items, planes // 2, 2, first_len // 2, 2, second_len // 2, 2)
    return -jnp.log(jnp.mean(blocks, axis=(2, 4, 6)))


def body(normals, plane_length, plane_amplitude, plane_mean):
    reals, planes, x_rows, y_cols = normals.shape
    x_parts = lax.axis_size("gx")
    y_parts = lax.axis_size("gy")
    total_x = x_rows * x_parts
    total_y = y_cols * y_parts
    wave_x, weight_x = cosine_weights(lax.axis_index("gx") * x_rows, x_rows, total_x)
    wave_y, weight_y = cosine_weights(lax.axis_index("gy") * y_cols, y_cols, total_y)
    radius = (wave_x / total_x)[:, None] ** 2 + (wave_y / total_y)[None, :] ** 2
    denominator = 1.0 + ((math.pi * plane_length) ** 2)[:, None, None] * radius[None]
    factor = (
        plane_amplitude * plane_length * (math.sqrt(2.0 * math.pi) / math.sqrt(total_x * total_y))
    )
    spectrum = factor[:, None, None] * jnp.power(denominator, -0.75)
    spectrum = spectrum * weight_x[None, :, None] * weight_y[None, None, :]
    scaled = normals * spectrum[None]
    y_outer = 64
    y_inner = total_y // y_outer
    cos_first_y, sin_first_y = first_tables(y_outer)
    cos_second_y, sin_second_y = second_tables(y_inner, y_outer)
    received = lax.all_to_all(scaled, "gy", split_axis=2, concat_axis=3, tiled=True)
    items, depth, row_count, line_len = received.shape
    blocks = received.reshape(items, depth, row_count, y_outer, y_inner)
    part_cos = jnp.einsum("rpxab,al->rpxbl", blocks, cos_first_y, precision=exactness)
    part_sin = jnp.einsum("rpxab,al->rpxbl", blocks, sin_first_y, precision=exactness)
    result_field = jnp.einsum("rpxbl,bhl->rpxhl", part_cos, cos_second_y, precision=exactness)
    result_field = result_field - jnp.einsum(
        "rpxbl,bhl->rpxhl", part_sin, sin_second_y, precision=exactness
    )
    result_field = result_field.reshape(items, depth, row_count, line_len)
    after_second = lax.all_to_all(result_field, "gy", split_axis=3, concat_axis=2, tiled=True)
    col_group = y_cols // x_parts
    cos_first_x, sin_first_x = first_tables(x_parts)
    cos_second_x, sin_second_x = second_tables(x_rows, x_parts)
    prepared = after_second.reshape(reals, planes, x_rows, x_parts, col_group)
    prepared = prepared.transpose(0, 1, 3, 4, 2).reshape(
        reals, planes, x_parts, 1, col_group * x_rows
    )
    received = lax.all_to_all(prepared, "gx", split_axis=2, concat_axis=3, tiled=True)
    items = received.shape[0]
    blocks = received.reshape(items, planes, x_parts, col_group, x_rows)
    items = blocks.shape[0]
    part_cos = jnp.einsum("rpjci,jl->rpcil", blocks, cos_first_x, precision=exactness)
    part_sin = jnp.einsum("rpjci,jl->rpcil", blocks, sin_first_x, precision=exactness)
    result_field = jnp.einsum("rpcil,ihl->rpchl", part_cos, cos_second_x, precision=exactness)
    result_field = result_field - jnp.einsum(
        "rpcil,ihl->rpchl", part_sin, sin_second_x, precision=exactness
    )
    result_field = result_field.reshape(items, planes, col_group, total_x)
    log_perm = result_field + plane_mean[None, :, None, None]
    items = log_perm.shape[0]
    sending = log_perm.reshape(items, planes, col_group, x_parts, x_rows)
    sending = sending.transpose(0, 1, 3, 2, 4).reshape(
        items, planes, x_parts, 1, col_group * x_rows
    )
    returned = lax.all_to_all(sending, "gx", split_axis=2, concat_axis=3, tiled=True)
    returned = returned.reshape(items, planes, x_parts, col_group, x_rows)
    regathered = returned.transpose(0, 1, 4, 2, 3).reshape(items, planes, x_rows, y_cols)
    return harmonic_log(regathered)


def solution(mesh):
    return jax.shard_map(
        body,
        mesh=mesh,
        in_specs=(P(None, None, "gx", "gy"), P(), P(), P()),
        out_specs=P(None, None, "gx", "gy"),
        check_vma=False,
    )
```

profile of v0, /device:TPU:1, one launch (start us, length us, event | category | flops | bytes accessed | tf_op | source)
XLA Modules:
  0.0 237.2 jit_solution(1629961647720667490)
XLA Ops:
  0.0 0.7 multiply_multiply_fusion.4
  0.7 0.1 broadcast_add_fusion
  0.8 1.2 multiply_multiply_fusion
  2.0 0.9 copy.67
  2.9 18.3 %all-to-all-start = ((f32[1,2,64,512]{3,1,0,2:T(2,128)}), f32[1,2,64,512]{3,1,0,2:T(2,128)S(1)}, u32[]{:S(2)}, u32[]{:S(2)}) async-start(f32[1,2,64,512]{3,1,0,2:T(2,128)} %copy.67), calls=%async_computation | async-start | bytes 524288 | tf_op jit(solution)/shard_map/all_to_all | solution.py:62
  21.2 15.5 %all-to-all-done = f32[1,2,64,512]{3,1,0,2:T(2,128)S(1)} async-done(((f32[1,2,64,512]{3,1,0,2:T(2,128)}), f32[1,2,64,512]{3,1,0,2:T(2,128)S(1)}, u32[]{:S(2)}, u32[]{:S(2)}) %all-to-all-start) | async-done | bytes 262176 | tf_op jit(solution)/shard_map/all_to_all | solution.py:62
  36.7 0.2 copy.99
  36.8 0.1 reshape.227
  37.0 1.0 fusion.41
  38.0 1.0 fusion.37
  39.0 0.5 copy.70
  39.5 1.4 copy.72
  40.9 13.5 %fusion.5 = f32[128,32,2,8]{1,3,2,0:T(8,128)S(1)} fusion(f32[2,8,64,128]{2,1,0,3:T(8,128)} %copy.72, s32[32,128]{0,1:T(8,128)S(1)} %multiply_add_fusion), kind=kOutput, calls=%fused_computation.8 | convolution fusion | flops 54001664 | bytes 802816 | tf_op jit(solution)/shard_map/rpxbl,bhl->rpxhl/dot_general | solution.py:68
  54.4 14.3 %fusion.17 = f32[1,2,8,32,128]{3,2,1,4,0:T(8,128)S(1)} fusion(f32[128,32,2,8]{1,3,2,0:T(8,128)S(1)} %fusion.5, f32[2,8,64,128]{2,1,0,3:T(8,128)S(1)} %copy.70, s32[32,128]{0,1:T(8,128)S(1)} %multiply_add_fusion), kind=kOutput, calls=%fused_computation.18 | convolution fusion | flops 54067200 | bytes 1064960 | tf_op jit(solution)/shard_map/rpxbl,bhl->rpxhl/dot_general | solution.py:67
  68.7 0.4 copy.73
  69.1 4.3 %copy.74 = f32[1,2,8,4096]{2,1,0,3:T(2,128)} copy(f32[1,2,8,4096]{3,0,2,1:T(1,128)S(1)} %bitcast.90) | data formatting | bytes 524288 | tf_op jit(solution)/shard_map/reshape | solution.py:71
  73.4 8.3 %reshape.240 = f32[8,1,8192]{2,1,0:T(1,128)S(1)} reshape(f32[4096,1,2,8]{3,2,1,0:T(2,128)} %bitcast.85) | data formatting | bytes 524288
  81.7 17.3 %all_to_all.48 = f32[8,1,8192]{2,1,0:T(1,128)S(1)} all-to-all(f32[8,1,8192]{2,1,0:T(1,128)S(1)} %reshape.240), channel_id=1, replica_groups=mesh['gx'=64,'gy'=8] {'gy'}, dimensions={0} | all-to-all | bytes 524288 | tf_op jit(solution)/shard_map/all_to_all | solution.py:72
  99.0 0.5 broadcast.307
  99.5 1.3 reduce.7
  100.7 8.3 %reshape.241 = f32[4096,1,2,8]{3,2,1,0:T(2,128)} reshape(f32[8,8192]{1,0:T(8,128)S(1)} %reduce.7) | data formatting | bytes 524288
  109.0 5.1 %copy.93 = f32[1,2,8,8,512]{4,2,3,1,0:T(8,128)S(1)} copy(f32[1,2,8,8,512]{2,1,4,3,0:T(2,128)} %bitcast.86) | data formatting | bytes 524288 | tf_op jit(solution)/shard_map/all_to_all | solution.py:72
  114.1 3.6 %reshape.229 = f32[1,2,64,64,8]{4,3,2,1,0:T(8,128)} reshape(f32[1,2,8,8,512]{4,3,2,1,0:T(8,128)S(1)} %bitcast.91) | data formatting | bytes 524288 | tf_op jit(solution)/shard_map/reshape | solution.py:76
  117.8 4.8 %copy.94 = f32[1,2,64,8,64]{4,3,1,2,0:T(8,128)S(1)} copy(f32[1,2,64,8,64]{3,2,4,1,0:T(8,128)} %bitcast.87) | data formatting | bytes 524288 | tf_op jit(solution)/shard_map/reshape | solution.py:77
  122.6 0.2 reshape.238
  122.8 40.0 %all_to_all.49 = f32[1,2,64,1,512]{4,1,3,0,2:T(2,128)S(1)} all-to-all(f32[1,2,64,1,512]{4,1,3,0,2:T(2,128)S(1)} %reshape.238), channel_id=1, replica_groups=mesh['gx'=64,'gy'=8] {'gx'}, dimensions={2} | all-to-all | bytes 524288 | tf_op jit(solution)/shard_map/all_to_all | solution.py:80
  162.8 0.2 copy.79
  163.1 0.7 fusion.39
  163.8 0.7 fusion.35
  164.5 0.5 copy.80
  165.0 1.4 copy.81
  166.4 13.5 %fusion.3 = f32[128,32,2,8]{1,3,2,0:T(8,128)S(1)} fusion(f32[2,8,64,128]{2,1,0,3:T(8,128)} %copy.81, s32[32,128]{0,1:T(8,128)S(1)} %multiply_add_fusion), kind=kOutput, calls=%fused_computation.6 | convolution fusion | flops 54001664 | bytes 802816 | tf_op jit(solution)/shard_map/rpcil,ihl->rpchl/dot_general | solution.py:87
  179.8 14.3 %fusion.23 = f32[1,2,8,32,128]{3,2,1,4,0:T(8,128)S(1)} fusion(f32[128,32,2,8]{1,3,2,0:T(8,128)S(1)} %fusion.3, f32[2,8,64,128]{2,1,0,3:T(8,128)S(1)} %copy.80, s32[32,128]{0,1:T(8,128)S(1)} %multiply_add_fusion), kind=kOutput, calls=%fused_computation.20 | convolution fusion | flops 54067200 | bytes 1064960 | tf_op jit(solution)/shard_map/rpcil,ihl->rpchl/dot_general | solution.py:86
  194.2 0.0 copy-start
  194.2 0.4 copy.82
  194.6 0.1 reshape.232
  194.8 0.1 copy-done
  194.8 0.1 add_bitcast_fusion
  195.0 0.3 copy.95
  195.3 0.2 reshape.239
  195.5 26.0 %all_to_all.50 = f32[1,2,64,1,512]{4,1,3,0,2:T(2,128)S(1)} all-to-all(f32[1,2,64,1,512]{4,1,3,0,2:T(2,128)S(1)} %reshape.239), channel_id=1, replica_groups=mesh['gx'=64,'gy'=8] {'gx'}, dimensions={2} | all-to-all | bytes 524288 | tf_op jit(solution)/shard_map/all_to_all | solution.py:97
  221.5 0.4 exponential_reduce_fusion
  221.8 0.1 reduce_sum.16
  221.9 10.0 %reduce_sum.23 = f32[32,2,256,2]{1,0,3,2:T(8,128)} reshape(f32[64,64,8]{0,2,1:T(8,128)S(1)} %bitcast.93) | data formatting | bytes 262144 | tf_op jit(solution)/shard_map/reduce_sum | solution.py:39
  232.0 4.5 %reduce_sum.24 = f32[32,256]{0,1:T(8,128)S(1)} reduce(f32[32,2,256,2]{1,0,3,2:T(8,128)} %reduce_sum.23, f32[]{:T(128)} %constant.77.clone.1), dimensions={1,3}, to_apply=%region_1.2 | reduce | flops 24576 | bytes 163844 | tf_op jit(solution)/shard_map/reduce_sum | solution.py:39
  236.6 0.7 copy.85
  (6 shorter events, 0.1 us)
Async XLA Ops:
  2.9 33.8 %all-to-all-start = ((f32[1,2,64,512]{3,1,0,2:T(2,128)}), f32[1,2,64,512]{3,1,0,2:T(2,128)S(1)}, u32[]{:S(2)}, u32[]{:S(2)}) async-start(f32[1,2,64,512]{3,1,0,2:T(2,128)} %copy.67), calls=%async_computation | async-start | bytes 524288 | tf_op jit(solution)/shard_map/all_to_all | solution.py:62
  194.2 0.7 copy-start
where the time goes:
time: 238 us; the launch traced here: 237 us
  blocking collectives  83.3 us (35%)
  matrix products  59 us (25%)
  local copies, waits for them, and re-layouts  52.7 us (22%)
  starting transfers between devices  18.3 us (8%)
  waiting for transfers between devices  15.5 us (7%)
  other arithmetic  8.27 us (3%)
    all_to_all x1, blocking collectives, body(): lax.all_to_all(prepared, 'gx', split_axis=2, concat_axis=3, tiled=True)  40 us
    all_to_all x1, blocking collectives, body(): lax.all_to_all(sending, 'gx', split_axis=2, concat_axis=3, tiled=True)  26 us
    all_to_all x1, starting transfers between devices, body(): lax.all_to_all(scaled, 'gy', split_axis=2, concat_axis=3, tiled=True)  18.3 us
    all_to_all x1, blocking collectives, body(): lax.all_to_all(result_field, 'gy', split_axis=3, concat_axis=2, tiled=True)  17.3 us
    unnamed x4, local copies, waits for them, and re-layouts  16.6 us
    all_to_all x1, waiting for transfers between devices, body(): lax.all_to_all(scaled, 'gy', split_axis=2, concat_axis=3, tiled=True)  15.5 us
    dot_general x1, matrix products, body(): jnp.einsum('rpxbl,bhl->rpxhl', part_cos, cos_second_y, precision=exactness)  14.3 us
    dot_general x1, matrix products, body(): jnp.einsum('rpcil,ihl->rpchl', part_cos, cos_second_x, precision=exactness)  14.3 us
  transfers between devices with their start and end apart: 1, of which 1 were waited for; matrix products, arithmetic and copies ran while one was open for 0% of the time, Pallas kernels for 0%

commit v1 on v0

v1 whole, which is shorter than its diff:
```python
import math

import jax
import jax.numpy as jnp
import numpy as np
from jax import lax
from jax.experimental import pallas as pl
from jax.experimental.pallas import tpu as pltpu
from jax.sharding import PartitionSpec as P

F32 = jnp.float32
BF16 = jnp.bfloat16
NX = 4096
NY = 4096
GX = 64
GY = 8
NN = (((1,), (0,)), ((), ()))
NT = (((1,), (1,)), ((), ()))
TN = (((0,), (0,)), ((), ()))


def np_split(table):
    high = table.astype(np.float32).astype(jnp.bfloat16)
    low = (table - high.astype(np.float64)).astype(np.float32).astype(jnp.bfloat16)
    return high, low


def split(values):
    high = values.astype(BF16)
    low = (values - high.astype(F32)).astype(BF16)
    return high, low


def mul(left, right, dims):
    return lax.dot_general(left, right, dims, preferred_element_type=F32)


def angles(top, period):
    return np.pi * (top % (2 * period)).astype(np.float64) / period


def y_tables():
    outer, inner = 32, 128
    a = np.arange(outer)[None, :]
    l = np.arange(outer)[:, None]
    first = angles(a * (2 * l + 1), 2 * outer)
    first = np.concatenate([np.cos(first), np.sin(first)], 0)
    high, low = np_split(first)
    first = np.concatenate([high, high, low], 1)
    b = np.arange(inner)[None, :]
    turn = angles(b * (2 * l + 1), 2 * NY)
    turn = np.stack([np.cos(turn), np.sin(turn)]).astype(np.float32)
    sub, j = np.meshgrid(np.arange(16), np.arange(GY), indexing="ij")
    m = np.where(sub < 8, 8 * j + sub, 127 - 8 * j - (sub - 8)).reshape(-1, 1)
    last = angles(2 * b * m, inner)
    last = np.concatenate([np.cos(last), -np.sin(last)], 1)
    return first, turn, np.concatenate(np_split(last), 0)


def x_tables():
    outer, inner = 512, 8
    l = np.concatenate([np.arange(0, 256, 2), np.arange(1, 256, 2)])[:, None]
    parts = []
    for odd in range(2):
        a = 2 * np.arange(256)[None, :] + odd
        phase = angles(a * (2 * l + 1), 2 * outer)
        parts.append(np.concatenate(np_split(np.concatenate([np.cos(phase), np.sin(phase)], 0)), 0))
    first = np.stack(parts)
    l = l[:, 0]
    rows = np.concatenate([l[:128], 511 - l[128:], l[128:], 511 - l[:128]])[:, None]
    lanes = np.arange(128)[None, :]
    b = lanes // 8 % 8
    turn = angles(b * (2 * rows + 1), 2 * NX)
    turn = np.stack([np.cos(turn), np.sin(turn)]).astype(np.float32)
    index = np.arange(128)[:, None]
    plane, fine = index // 64, index // 8 % 4 * 2 + index // 32 % 2
    m = np.array([0, 1, 2, 3, 7, 6, 5, 4])[index % 8]
    same = 1.0 * ((lanes // 64 == plane) & (lanes % 8 == fine))
    phase = angles(2 * b * m, inner)
    last = np.concatenate([same * np.cos(phase), -same * np.sin(phase)], 1)
    return first, turn, np.concatenate(np_split(last), 0)


def place_table():
    src = np.arange(GX)
    octet, sub = src // 16, src % 16
    table = np.zeros((GX, 4, 256), np.float32)
    for ly in range(4):
        column = np.where(sub < 8, 32 * sub + 4 * octet + ly, 32 * (sub - 8) + 31 - 4 * octet - ly)
        table[src, ly, column] = 1
    return np.concatenate([table.reshape(GX, 1024)] * 3, 0).astype(jnp.bfloat16)


def scale_kernel(ids, length, amplitude, x_ref, o_ref):
    norming = math.sqrt(2.0 * math.pi) / math.sqrt(NX * NY)
    row = ids[0] * 64 + lax.broadcasted_iota(jnp.int32, (64, 128), 0)
    row_wave = row.astype(F32) * (1.0 / NX)
    row_weight = jnp.where(row == 0, math.sqrt(1.0 / NX), math.sqrt(2.0 / NX))
    for c in range(4):
        col = ids[1] * 512 + c * 128 + lax.broadcasted_iota(jnp.int32, (64, 128), 1)
        col_wave = col.astype(F32) * (1.0 / NY)
        weight = row_weight * jnp.where(col == 0, math.sqrt(1.0 / NY), math.sqrt(2.0 / NY))
        radius = row_wave * row_wave + col_wave * col_wave
        for p in range(2):
            reach = math.pi * length[p]
            root = lax.rsqrt(1.0 + reach * reach * radius)
            factor = amplitude[p] * length[p] * norming
            spectrum = factor * (root * jnp.sqrt(root))
            scaled = x_ref[0, p, :, c * 128:(c + 1) * 128] * spectrum * weight
            o_ref[:, c, p] = scaled.reshape(8, 8, 128)


def y_kernel(x_ref, first_ref, turn_ref, last_ref, o_ref, w_ref):
    pieces = []
    for line in range(16):
        high, low = split(x_ref[pl.ds(line, 32, stride=16), :])
        pieces.append(jnp.concatenate([high, low, high], 0))
    part = mul(first_ref[...], jnp.concatenate(pieces, 1), NN)
    turn_c, turn_s = turn_ref[0], turn_ref[1]
    for line in range(16):
        block = part[:, line * 128:(line + 1) * 128]
        part_c, part_s = block[:32], block[32:]
        w_ref[:, line, :, :128] = (part_c * turn_c - part_s * turn_s).reshape(4, 8, 128)
        w_ref[:, line, :, 128:] = (part_c * turn_s + part_s * turn_c).reshape(4, 8, 128)
    high, low = split(w_ref[...].reshape(512, 256))
    both = mul(last_ref[...], high, NT)
    out = both[:128] + both[128:] + mul(last_ref[:128, :], low, NT)
    for octet in range(4):
        o_ref[octet * 128:(octet + 1) * 128, :] = out[:, octet * 128:(octet + 1) * 128]


def x_kernel(mean, x_ref, first_ref, turn_ref, last_ref, o_ref):
    halves = []
    for odd in range(2):
        values = x_ref[pl.ds(odd, 256, stride=2), :]
        both = mul(first_ref[odd], jnp.concatenate(split(values), 1), NN)
        halves.append(both[:512, :128] + (both[:512, 128:] + both[512:, :128]))
    (even_c, even_s), (odd_c, odd_s) = [(h[:256], h[256:]) for h in halves]
    plus_c, minus_c = even_c + odd_c, even_c - odd_c
    plus_s, minus_s = even_s + odd_s, odd_s - even_s
    part_c = jnp.concatenate([plus_c[:128], minus_c[128:], plus_c[128:], minus_c[:128]], 0)
    part_s = jnp.concatenate([plus_s[:128], minus_s[128:], plus_s[128:], minus_s[:128]], 0)
    turn_c, turn_s = turn_ref[0], turn_ref[1]
    turned = jnp.concatenate(
        [part_c * turn_c - part_s * turn_s, part_c * turn_s + part_s * turn_c], 1
    )
    high, low = split(turned)
    both = mul(last_ref[...], high, NT)
    field = both[:128] + both[128:] + mul(last_ref[:128, :], low, NT)
    total = jnp.zeros((32, 512), F32)
    for p in range(2):
        values = jnp.exp(-(field[64 * p:64 * p + 64] + mean[p]))
        total = total + values[:32] + values[32:]
    coarse = -jnp.log((total[:, :256] + total[:, 256:]) * 0.125)
    group = lax.broadcasted_iota(jnp.int32, (8, 128), 1) // 32
    for half in range(2):
        blocks = [coarse[8 * ly:8 * ly + 8, 128 * half:128 * half + 128] for ly in range(4)]
        for q in range(4):
            row = blocks[q]
            for ly in range(4):
                if ly != q:
                    row = jnp.where(group == ly, pltpu.roll(blocks[ly], (ly - q) * 32 % 128, 1), row)
            block = 7 - q if half else q
            o_ref[:, block, :] = row[:4]
            o_ref[:, 15 - block, :] = row[4:]


def place_kernel(ids, x_ref, table_ref, o_ref):
    values = x_ref[...]
    high, rest = values.astype(BF16), values - values.astype(BF16).astype(F32)
    middle, low = split(rest)
    spread = mul(jnp.concatenate([high, middle, low], 0), table_ref[...], TN)
    out = spread[:32, :256]
    for ly in range(1, 4):
        out = out + spread[32 * ly:32 * ly + 32, 256 * ly:256 * ly + 256]
    back = ids[0] // 4 % 2
    for r in range(32):
        o_ref[pl.ds(jnp.where(back == 1, 31 - r, r), 1), :] = out[r:r + 1]


def call(kernel, shape, places, scratch=(), cost=None):
    spaces = {"s": pltpu.SMEM, "v": pltpu.VMEM}
    return pl.pallas_call(
        kernel,
        out_shape=jax.ShapeDtypeStruct(shape, F32),
        in_specs=[pl.BlockSpec(memory_space=spaces[place]) for place in places],
        out_specs=pl.BlockSpec(memory_space=pltpu.VMEM),
        scratch_shapes=list(scratch),
        compiler_params=pltpu.CompilerParams(vmem_limit_bytes=32 * 1024 * 1024),
    )


def body(normals, plane_length, plane_amplitude, plane_mean):
    ids = jnp.stack([lax.axis_index("gx"), lax.axis_index("gy")]).astype(jnp.int32)
    scaled = call(scale_kernel, (8, 4, 2, 8, 128), "sssv")(
        ids, plane_length, plane_amplitude, normals
    )
    lines = lax.all_to_all(scaled.reshape(8, 64, 128), "gy", 0, 0, tiled=True)
    first, turn, last = y_tables()
    rows = call(y_kernel, (512, 128), "vvvv", [pltpu.VMEM((4, 16, 8, 256), F32)])(
        lines.reshape(512, 128), first, turn, last
    )
    rows = lax.all_to_all(rows.reshape(512, 1, 128), ("gx", "gy"), 0, 0, tiled=True)
    first, turn, last = x_tables()
    coarse = call(x_kernel, (4, 16, 128), "svvvv")(
        plane_mean, rows.reshape(512, 128), first, turn, last
    )
    coarse = lax.all_to_all(coarse.reshape(64, 1, 128), "gx", 0, 0, tiled=True)
    out = call(place_kernel, (32, 256), "svv")(ids, coarse.reshape(64, 128), place_table())
    return out.reshape(1, 1, 32, 256)


def solution(mesh):
    return jax.shard_map(
        body,
        mesh=mesh,
        in_specs=(P(None, None, "gx", "gy"), P(), P(), P()),
        out_specs=P(None, None, "gx", "gy"),
        check_vma=False,
    )
```

time: 238 us -> 104 us (0.44)
  matrix products: 59 us -> 0 us
  local copies, waits for them, and re-layouts: 52.7 us -> 3.88 us
  starting transfers between devices: 18.3 us -> 0 us
  waiting for transfers between devices: 15.5 us -> 0 us
  blocking collectives: 83.3 us -> 95.2 us
  other arithmetic: 8.27 us -> 0.08 us
  Pallas kernels: 0 us -> 4.01 us
    dot_general x8 -> x0, matrix products: 59 us -> none  [the longest x1 14.3 us: body(): jnp.einsum('rpxbl,bhl->rpxhl', part_cos, cos_second_y, precision=exactness)]
    all_to_all x1 -> x0, starting transfers between devices: 18.3 us -> none  [body(): lax.all_to_all(scaled, 'gy', split_axis=2, concat_axis=3, tiled=True)]
    all_to_all x1 -> x0, waiting for transfers between devices: 15.5 us -> none  [body(): lax.all_to_all(scaled, 'gy', split_axis=2, concat_axis=3, tiled=True)]
    reshape x7 -> x0, local copies, waits for them, and re-layouts: 13.6 us -> none  [the longest x2 5.06 us: body(): prepared.transpose(0, 1, 3, 4, 2)]
    unnamed x4 -> x22, local copies, waits for them, and re-layouts: 16.6 us -> 3.88 us
    all_to_all x3, blocking collectives: 83.3 us -> 95.2 us  [the longest x1 44.5 us: body(): lax.all_to_all(rows.reshape(512, 1, 128), ('gx', 'gy'), 0, 0, tiled=True)]
    reduce_sum x2 -> x0, local copies, waits for them, and re-layouts: 10.1 us -> none  [harmonic_log(): return -jnp.log(jnp.mean(blocks, axis=(2, 4, 6)))]
    all_to_all x4 -> x0, local copies, waits for them, and re-layouts: 6 us -> none  [the longest x2 5.63 us: body(): lax.all_to_all(result_field, 'gy', split_axis=3, concat_axis=2, tiled=True)]
  transfers between devices with their start and end apart: 1 -> 0, of which waited for: 1 -> 0; matrix products, arithmetic and copies ran while one was open for 0% -> 0% of each run, Pallas kernels for 0% -> 0%
where the time goes in v1:
time: 104 us; the launch traced here: 103 us
  blocking collectives  95.2 us (92%)
  Pallas kernels  4.01 us (4%)
  local copies, waits for them, and re-layouts  3.88 us (4%)
    all_to_all x1, blocking collectives, body(): lax.all_to_all(rows.reshape(512, 1, 128), ('gx', 'gy'), 0, 0, tiled=True)  44.5 us
    all_to_all x1, blocking collectives, body(): lines = lax.all_to_all(scaled.reshape(8, 64, 128), 'gy', 0, 0, tiled=True)  33.6 us
    all_to_all x1, blocking collectives, body(): coarse = lax.all_to_all(coarse.reshape(64, 1, 128), 'gx', 0, 0, tiled=True)  17.1 us
    unnamed x22, local copies, waits for them, and re-layouts  3.88 us

profile of v1, /device:TPU:1, one launch (start us, length us, event | category | flops | bytes accessed | tf_op | source)
XLA Modules:
  0.0 103.2 jit_solution(8234313499735658000)
XLA Ops:
  0.0 0.0 copy-start.7
  0.0 0.0 copy-start.8
  0.0 0.0 copy-start.9
  0.0 0.1 pad_add_fusion.ids
  0.1 0.6 copy-done.8
  0.7 0.0 copy-done.9
  0.7 0.0 copy-start.3
  0.7 0.9 copy-done.3
  1.6 0.0 copy-start
  1.6 0.7 shard_map.109
  2.3 33.6 %all_to_all.15 = f32[8,64,128]{2,1,0:T(8,128)S(1)} all-to-all(f32[8,64,128]{2,1,0:T(8,128)S(1)} %bitcast.14), channel_id=1, replica_groups=mesh['gx'=64,'gy'=8] {'gy'}, dimensions={0} | all-to-all | bytes 524288 | tf_op jit(solution)/shard_map/all_to_all | solution.py:198
  36.0 0.0 copy-done.7
  36.0 0.0 copy-start.5
  36.0 0.9 copy-done.5
  36.9 0.0 copy-start.6
  36.9 0.8 copy-done.6
  37.6 0.0 copy-start.1
  37.6 0.5 shard_map.110
  38.1 0.0 copy-start.4
  38.2 44.5 %all_to_all.16 = f32[512,1,128]{2,1,0:T(1,128)S(1)} all-to-all(f32[512,1,128]{2,1,0:T(1,128)S(1)} %bitcast.16), channel_id=1, replica_groups=mesh['gx'=64,'gy'=8] {'gx','gy'}, dimensions={0} | all-to-all | bytes 524288 | tf_op jit(solution)/shard_map/all_to_all | solution.py:203
  82.6 0.0 copy-start.10
  82.6 0.0 copy-done
  82.6 0.0 copy-done.1
  82.6 0.0 copy-done.4
  82.6 0.6 copy-done.10
  83.3 0.0 copy-start.2
  83.3 1.4 %shard_map.111 = f32[4,16,128]{2,1,0:T(8,128)S(1)} custom-call(f32[2]{0:T(128)S(1)} %copy-done.10, f32[512,128]{1,0:T(8,128)S(1)} %bitcast.13, bf16[2,1024,256]{2,1,0:T(8,128)(2,1)S(1)} %copy-done, f32[2,512,128]{2,1,0:T(8,128)S(1)} %copy-done.1, bf16[256,256]{1,0:T(8,128)(2,1)S(1)} %copy-done.4), custom_call_target="tpu_custom_call" | custom-call | tf_op jit(solution)/shard_map/pallas_call | solution.py:205
  84.7 17.1 %all_to_all.17 = f32[64,1,128]{2,1,0:T(1,128)S(1)} all-to-all(f32[64,1,128]{2,1,0:T(1,128)S(1)} %bitcast.17), channel_id=1, replica_groups=mesh['gx'=64,'gy'=8] {'gx'}, dimensions={0} | all-to-all | bytes 65536 | tf_op jit(solution)/shard_map/all_to_all | solution.py:208
  101.8 0.0 copy-done.2
  101.8 1.4 %shard_map.112 = f32[32,256]{1,0:T(8,128)} custom-call(s32[2]{0:T(128)S(1)} %pad_add_fusion.ids, f32[64,128]{1,0:T(8,128)S(1)} %bitcast.18, bf16[192,1024]{1,0:T(8,128)(2,1)S(1)} %copy-done.2), custom_call_target="tpu_custom_call" | custom-call | tf_op jit(solution)/shard_map/pallas_call | solution.py:209
Async XLA Ops:
  0.0 36.0 %copy-start.7 = (bf16[64,96]{1,0:T(8,128)(2,1)S(1)}, bf16[64,96]{1,0:T(8,128)(2,1)}, u32[]{:S(2)}) copy-start(bf16[64,96]{1,0:T(8,128)(2,1)} %constant.23.clone.first_ref) | copy-start | bytes 36868
  0.0 0.7 copy-start.8
  0.0 0.7 copy-start.9
  0.7 0.9 copy-start.3
  1.6 81.0 %copy-start = (bf16[2,1024,256]{2,1,0:T(8,128)(2,1)S(1)}, bf16[2,1024,256]{2,1,0:T(8,128)(2,1)}, u32[]{:S(2)}) copy-start(bf16[2,1024,256]{2,1,0:T(8,128)(2,1)} %constant.26.clone.first_ref) | copy-start | bytes 3145732
  36.0 0.9 copy-start.5
  36.9 0.8 copy-start.6
  37.6 45.0 %copy-start.1 = (f32[2,512,128]{2,1,0:T(8,128)S(1)}, f32[2,512,128]{2,1,0:T(8,128)}, u32[]{:S(2)}) copy-start(f32[2,512,128]{2,1,0:T(8,128)} %constant.27.clone.turn_ref) | copy-start | bytes 1572868
  38.1 44.5 %copy-start.4 = (bf16[256,256]{1,0:T(8,128)(2,1)S(1)}, bf16[256,256]{1,0:T(8,128)(2,1)}, u32[]{:S(2)}) copy-start(bf16[256,256]{1,0:T(8,128)(2,1)} %constant.28.clone.last_ref) | copy-start | bytes 393220
  82.6 0.7 copy-start.10
  83.3 18.5 %copy-start.2 = (bf16[192,1024]{1,0:T(8,128)(2,1)S(1)}, bf16[192,1024]{1,0:T(8,128)(2,1)}, u32[]{:S(2)}) copy-start(bf16[192,1024]{1,0:T(8,128)(2,1)} %constant.29.clone.table_ref) | copy-start | bytes 1179652

commit v2 on v1

v2 whole, which is shorter than its diff:
```python
import math

import jax
import jax.numpy as jnp
import numpy as np
from jax import lax
from jax.experimental import pallas as pl
from jax.experimental.pallas import tpu as pltpu
from jax.sharding import PartitionSpec as P

F32 = jnp.float32
BF16 = jnp.bfloat16
NX = 4096
NY = 4096
GX = 64
GY = 8
NN = (((1,), (0,)), ((), ()))
NT = (((1,), (1,)), ((), ()))
TN = (((0,), (0,)), ((), ()))


def np_split(table):
    high = table.astype(np.float32).astype(jnp.bfloat16)
    low = (table - high.astype(np.float64)).astype(np.float32).astype(jnp.bfloat16)
    return high, low


def split(values):
    high = values.astype(BF16)
    low = (values - high.astype(F32)).astype(BF16)
    return high, low


def mul(left, right, dims):
    return lax.dot_general(left, right, dims, preferred_element_type=F32)


def angles(top, period):
    return np.pi * (top % (2 * period)).astype(np.float64) / period


def y_tables():
    outer, inner = 32, 128
    a = np.arange(outer).reshape(4, 2, 4).transpose(1, 0, 2).reshape(1, outer)
    l = np.arange(outer)[:, None]
    phase = angles(a * (2 * l + 1), 2 * outer)
    high, low = [t.astype(np.float64) for t in np_split(np.concatenate([np.cos(phase), np.sin(phase)], 0))]
    b = np.arange(inner)[None, :]
    turn = angles(b * (2 * l + 1), 2 * NY)
    turn = np.concatenate([np.cos(turn), np.sin(turn)], 1)
    sub, j = np.meshgrid(np.arange(16), np.arange(GY), indexing="ij")
    m = np.where(sub < 8, 8 * j + sub, 127 - 8 * j - (sub - 8)).reshape(-1, 1)
    last = angles(2 * b * m, inner)
    last = np.concatenate([np.cos(last), -np.sin(last)], 1)
    packed = np.zeros((288, 256))
    for h in range(2):
        own = slice(16 * h, 16 * h + 16)
        packed[64 * h:64 * h + 64, :48] = np.concatenate([high[:, own], high[:, own], low[:, own]], 1)
    packed[128:160] = turn
    packed[160:] = last
    return packed.astype(np.float32)


def x_tables():
    outer, inner = 256, 16
    l = np.concatenate([np.arange(0, outer, 2), np.arange(1, outer, 2)])[:, None]
    phase = angles(np.arange(outer)[None, :] * (2 * l + 1), 2 * outer)
    first = np.concatenate(np_split(np.concatenate([np.cos(phase), np.sin(phase)], 0)), 0)
    lanes = np.arange(128)[None, :]
    b = lanes // 8
    turn = angles(b * (2 * l + 1), 2 * NX)
    turn = np.stack([np.cos(turn), np.sin(turn)]).astype(np.float32)
    index = np.arange(128)[:, None]
    fine = index // 16 % 4 * 2 + index // 64
    m = np.concatenate([np.arange(8), np.arange(15, 7, -1)])[index % 16]
    same = 1.0 * (lanes % 8 == fine)
    phase = angles(2 * b * m, inner)
    last = np.concatenate([same * np.cos(phase), -same * np.sin(phase)], 1)
    return first, turn, np.concatenate(np_split(last), 0)


def place_table():
    src = np.arange(GX)
    octet, sub = src // 16, src % 16
    table = np.zeros((GX, 4, 256), np.float32)
    for ly in range(4):
        column = np.where(sub < 8, 32 * sub + 4 * octet + ly, 32 * (sub - 8) + 31 - 4 * octet - ly)
        table[src, ly, column] = 1
    return np.concatenate([table.reshape(GX, 1024)] * 3, 0).astype(jnp.bfloat16)


def scale_kernel(ids, length_in, amplitude_in, mean_in, x_in, o_ref, mean_ref, length, amplitude, mean, x_ref, sems):
    moves = [
        pltpu.make_async_copy(source, target, sems.at[k])
        for k, (source, target) in enumerate(
            [(x_in, x_ref), (length_in, length), (amplitude_in, amplitude), (mean_in, mean)]
        )
    ]
    for move in moves:
        move.start()
    norming = math.sqrt(2.0 * math.pi) / math.sqrt(NX * NY)
    row = ids[0] * 64 + lax.broadcasted_iota(jnp.int32, (64, 128), 0)
    row_wave = row.astype(F32) * (1.0 / NX)
    row_wave = row_wave * row_wave
    row_weight = jnp.where(row == 0, math.sqrt(1.0 / NX), math.sqrt(2.0 / NX))
    for move in moves:
        move.wait()
    for c in range(4):
        col = ids[1] * 512 + c * 128 + lax.broadcasted_iota(jnp.int32, (64, 128), 1)
        col_wave = col.astype(F32) * (1.0 / NY)
        weight = row_weight * jnp.where(col == 0, math.sqrt(1.0 / NY), math.sqrt(2.0 / NY))
        radius = row_wave + col_wave * col_wave
        for p in range(2):
            reach = math.pi * length[p]
            root = lax.rsqrt(1.0 + reach * reach * radius)
            factor = amplitude[p] * length[p] * norming
            spectrum = factor * (root * jnp.sqrt(root))
            scaled = x_ref[0, p, :, c * 128:(c + 1) * 128] * spectrum * weight
            o_ref[:, c, p] = scaled.reshape(4, 16, 128)
    for p in range(2):
        mean_ref[p] = jnp.full((8, 128), mean[p], F32)


def y_kernel(ids, x_ref, table_ref, o_ref, w_ref):
    half = ids[1] % 2
    first = table_ref[pl.ds(pl.multiple_of(half * 64, 64), 64), :128].astype(BF16)[:, :48]
    turn_c, turn_s = table_ref[128:160, :128], table_ref[128:160, 128:]
    last = jnp.concatenate(split(table_ref[160:288, :]), 0)
    for group in range(4):
        pieces = []
        for line in range(8 * group, 8 * group + 8):
            high, low = split(x_ref[pl.ds(line, 16, stride=32), :])
            pieces.append(jnp.concatenate([high, low, high], 0))
        part = mul(first, jnp.concatenate(pieces, 1), NN)
        for k in range(8):
            part_c, part_s = part[:32, k * 128:(k + 1) * 128], part[32:, k * 128:(k + 1) * 128]
            line = 8 * group + k
            w_ref[:, line, :, :128] = (part_c * turn_c - part_s * turn_s).reshape(4, 8, 128)
            w_ref[:, line, :, 128:] = (part_c * turn_s + part_s * turn_c).reshape(4, 8, 128)
    for octet in range(4):
        high, low = split(w_ref[octet].reshape(256, 256))
        both = mul(last, high, NT)
        out = both[:128] + both[128:] + mul(last[:128], low, NT)
        for p in range(2):
            o_ref[pl.ds(octet * 256 + p, 128, stride=2), :] = out[:, p * 128:(p + 1) * 128]


def x_kernel(mean_ref, x_ref, first_ref, turn_ref, last_ref, o_ref):
    total = jnp.zeros((64, 128), F32)
    turn_c, turn_s = turn_ref[0], turn_ref[1]
    for p in range(2):
        values = x_ref[pl.ds(p, 256, stride=4), :] + x_ref[pl.ds(p + 2, 256, stride=4), :]
        both = mul(first_ref[...], jnp.concatenate(split(values), 1), NN)
        part = both[:512, :128] + (both[:512, 128:] + both[512:, :128])
        part_c, part_s = part[:256], part[256:]
        turned = jnp.concatenate(
            [part_c * turn_c - part_s * turn_s, part_c * turn_s + part_s * turn_c], 1
        )
        high, low = split(turned)
        both = mul(last_ref[...], high, NT)
        field = both[:128] + both[128:] + mul(last_ref[:128, :], low, NT)
        for side in range(2):
            values = jnp.exp(-(field[:, 128 * side:128 * side + 128] + mean_ref[p, 0:1, :]))
            total = total + values[:64] + values[64:]
    coarse = -jnp.log(total * 0.125)
    group = lax.broadcasted_iota(jnp.int32, (16, 128), 1) // 32
    blocks = [coarse[16 * ly:16 * ly + 16] for ly in range(4)]
    for q in range(4):
        row = blocks[q]
        for ly in range(4):
            if ly != q:
                row = jnp.where(group == ly, pltpu.roll(blocks[ly], (ly - q) * 32 % 128, 1), row)
        o_ref[:, q, :] = row[:8]
        o_ref[:, 7 - q, :] = row[8:]


def place_kernel(ids, x_ref, table_ref, o_ref):
    values = x_ref[...]
    high, rest = values.astype(BF16), values - values.astype(BF16).astype(F32)
    middle, low = split(rest)
    spread = mul(jnp.concatenate([high, middle, low], 0), table_ref[...], TN)
    out = spread[:32, :256]
    for ly in range(1, 4):
        out = out + spread[32 * ly:32 * ly + 32, 256 * ly:256 * ly + 256]
    back = ids[0] // 4 % 2
    for r in range(32):
        o_ref[pl.ds(jnp.where(back == 1, 31 - r, r), 1), :] = out[r:r + 1]


def call(kernel, shapes, places, scratch=()):
    spaces = {"s": pltpu.SMEM, "v": pltpu.VMEM, "h": pltpu.HBM}
    outs = [jax.ShapeDtypeStruct(shape, F32) for shape in shapes]
    result = pl.pallas_call(
        kernel,
        out_shape=outs,
        in_specs=[pl.BlockSpec(memory_space=spaces[place]) for place in places],
        out_specs=[pl.BlockSpec(memory_space=pltpu.VMEM)] * len(outs),
        scratch_shapes=list(scratch),
        compiler_params=pltpu.CompilerParams(vmem_limit_bytes=32 * 1024 * 1024),
    )
    return lambda *operands: result(*operands)


def body(normals, plane_length, plane_amplitude, plane_mean):
    ids = jnp.stack([lax.axis_index("gx"), lax.axis_index("gy")]).astype(jnp.int32)
    scratch = [pltpu.SMEM((2,), F32)] * 3 + [pltpu.VMEM((1, 2, 64, 512), F32), pltpu.SemaphoreType.DMA((4,))]
    scaled, mean = call(scale_kernel, [(4, 4, 2, 16, 128), (2, 8, 128)], "shhhh", scratch)(
        ids, plane_length, plane_amplitude, plane_mean, normals
    )
    sides = [[2 * y + h for y in range(4)] for h in range(2)]
    lines = lax.all_to_all(
        scaled.reshape(4, 128, 128), "gy", 0, 0, tiled=True, axis_index_groups=sides
    )
    (rows,) = call(y_kernel, [(1024, 128)], "svv", [pltpu.VMEM((4, 32, 8, 256), F32)])(
        ids, lines.reshape(512, 128), y_tables()
    )
    rows = lax.all_to_all(rows.reshape(512, 2, 128), ("gx", "gy"), 0, 0, tiled=True)
    first, turn, last = x_tables()
    (coarse,) = call(x_kernel, [(8, 8, 128)], "vvvvv")(
        mean, rows.reshape(1024, 128), first, turn, last
    )
    coarse = lax.all_to_all(coarse.reshape(64, 1, 128), "gx", 0, 0, tiled=True)
    (out,) = call(place_kernel, [(32, 256)], "svv")(ids, coarse.reshape(64, 128), place_table())
    return out.reshape(1, 1, 32, 256)


def solution(mesh):
    return jax.shard_map(
        body,
        mesh=mesh,
        in_specs=(P(None, None, "gx", "gy"), P(), P(), P()),
        out_specs=P(None, None, "gx", "gy"),
        check_vma=False,
    )
```

time: 104 us -> 93.3 us (0.90)
  blocking collectives: 95.2 us -> 86 us
  local copies, waits for them, and re-layouts: 3.88 us -> 1.59 us
  Pallas kernels: 4.01 us -> 5.27 us
    all_to_all x2, blocking collectives: 78.1 us -> 69.1 us  [the longest x1 58.7 us: body(): lax.all_to_all(rows.reshape(512, 2, 128), ('gx', 'gy'), 0, 0, tiled=True)]
    unnamed x22 -> x18, local copies, waits for them, and re-layouts: 3.88 us -> 1.59 us
    pallas_call x4, Pallas kernels: 4.01 us -> 5.27 us  [call(): return lambda *operands: result(*operands)]
where the time goes in v2:
time: 93.3 us; the launch traced here: 93 us
  blocking collectives  86 us (92%)
  Pallas kernels  5.27 us (6%)
  local copies, waits for them, and re-layouts  1.59 us (2%)
    all_to_all x1, blocking collectives, body(): lax.all_to_all(rows.reshape(512, 2, 128), ('gx', 'gy'), 0, 0, tiled=True)  58.7 us
    all_to_all x1, blocking collectives, body(): coarse = lax.all_to_all(coarse.reshape(64, 1, 128), 'gx', 0, 0, tiled=True)  16.9 us
    all_to_all x1, blocking collectives, body(): lax.all_to_all(scaled.reshape(4, 128, 128), 'gy', 0, 0, tiled=True, axis_...  10.5 us
    pallas_call x4, Pallas kernels, call(): return lambda *operands: result(*operands)  5.27 us

profile of v2, /device:TPU:1, one launch (start us, length us, event | category | flops | bytes accessed | tf_op | source)
XLA Modules:
  0.0 93.0 jit_solution(7170896908406688407)
XLA Ops:
  0.0 0.0 copy-start.6
  0.0 0.0 copy-start.7
  0.0 0.0 copy-start.8
  0.0 0.1 pad_add_fusion.ids
  0.1 0.6 copy-done.6
  0.7 0.0 copy-done.7
  0.7 0.0 copy-done.8
  0.7 0.0 copy-start.3
  0.7 0.9 %copy-done.3 = f32[1,2,64,512]{3,2,1,0:T(8,128)S(1)} copy-done((f32[1,2,64,512]{3,2,1,0:T(8,128)S(1)}, f32[1,2,64,512]{3,2,1,0:T(8,128)}, u32[]{:S(2)}) %copy-start.3) | copy-done | bytes 262168
  1.6 1.3 %shard_map.91 = (f32[4,4,2,16,128]{4,3,2,1,0:T(8,128)S(1)}, f32[2,8,128]{2,1,0:T(8,128)S(1)}) custom-call(s32[2]{0:T(128)S(1)} %pad_add_fusion.ids, f32[2]{0:T(128)S(1)} %copy-done.6, f32[2]{0:T(128)S(1)} %copy-done.7, f32[2]{0:T(128)S(1)} %copy-done.8, f32[1,2,64,512]{3,2,1,0:T(8,128)S(1)} %copy-done.3), custom_call_target="tpu_custom_call" | custom-call | tf_op jit(solution)/shard_map/pallas_call | solution.py:201
  2.9 0.0 copy-start.2
  3.0 10.5 %all_to_all.15 = f32[4,128,128]{2,1,0:T(8,128)S(1)} all-to-all(f32[4,128,128]{2,1,0:T(8,128)S(1)} %bitcast.14), channel_id=1, replica_groups={{0,2,4,6},{1,3,5,7},{8,10,12,14},{9,11,13,15},{16,18,20,22},{17,19,21,2..., dimensions={0} | all-to-all | bytes 524288 | tf_op jit(solution)/shard_map/all_to_all | solution.py:211
  13.4 0.0 copy-done.2
  13.4 1.3 %shard_map.92 = f32[1024,128]{1,0:T(8,128)S(1)} custom-call(s32[2]{0:T(128)S(1)} %pad_add_fusion.ids, f32[512,128]{1,0:T(8,128)S(1)} %bitcast.13, f32[288,256]{1,0:T(8,128)S(1)} %copy-done.2), custom_call_target="tpu_custom_call" | custom-call | tf_op jit(solution)/shard_map/pallas_call | solution.py:201
  14.7 0.0 copy-start
  14.7 0.0 copy-start.4
  14.7 0.0 copy-start.5
  14.8 58.7 %all_to_all.16 = f32[512,2,128]{2,1,0:T(2,128)S(1)} all-to-all(f32[512,2,128]{2,1,0:T(2,128)S(1)} %bitcast.12), channel_id=1, replica_groups=mesh['gx'=64,'gy'=8] {'gx','gy'}, dimensions={0} | all-to-all | bytes 1048576 | tf_op jit(solution)/shard_map/all_to_all | solution.py:217
  73.4 0.0 copy-done
  73.4 0.0 copy-done.4
  73.4 0.0 copy-done.5
  73.4 0.0 copy-start.1
  73.4 1.3 %shard_map.93 = f32[8,8,128]{2,1,0:T(8,128)S(1)} custom-call(f32[2,8,128]{2,1,0:T(8,128)S(1)} %get-tuple-element.7.mean_ref, f32[1024,128]{1,0:T(8,128)S(1)} %bitcast.11, bf16[1024,256]{1,0:T(8,128)(2,1)S(1)} %copy-done, f32[2,256,128]{2,1,0:T(8,128)S(1)} %copy-done.4, bf16[256,256]{1,0:T(8,128)(2,1)S(1)} %copy-done.5), custom_call_target="tpu_custom_call" | custom-call | tf_op jit(solution)/shard_map/pallas_call | solution.py:201
  74.7 16.9 %all_to_all.17 = f32[64,1,128]{2,1,0:T(1,128)S(1)} all-to-all(f32[64,1,128]{2,1,0:T(1,128)S(1)} %bitcast.15), channel_id=1, replica_groups=mesh['gx'=64,'gy'=8] {'gx'}, dimensions={0} | all-to-all | bytes 65536 | tf_op jit(solution)/shard_map/all_to_all | solution.py:222
  91.6 0.0 copy-done.1
  91.6 1.4 %shard_map.94 = f32[32,256]{1,0:T(8,128)} custom-call(s32[2]{0:T(128)S(1)} %pad_add_fusion.ids, f32[64,128]{1,0:T(8,128)S(1)} %bitcast.16, bf16[192,1024]{1,0:T(8,128)(2,1)S(1)} %copy-done.1), custom_call_target="tpu_custom_call" | custom-call | tf_op jit(solution)/shard_map/pallas_call | solution.py:201
Async XLA Ops:
  0.0 0.7 copy-start.6
  0.0 0.7 copy-start.7
  0.0 0.7 copy-start.8
  0.7 0.9 %copy-start.3 = (f32[1,2,64,512]{3,2,1,0:T(8,128)S(1)}, f32[1,2,64,512]{3,2,1,0:T(8,128)}, u32[]{:S(2)}) copy-start(f32[1,2,64,512]{3,2,1,0:T(8,128)} %x_in.1) | copy-start | bytes 786436
  2.9 10.5 %copy-start.2 = (f32[288,256]{1,0:T(8,128)S(1)}, f32[288,256]{1,0:T(8,128)}, u32[]{:S(2)}) copy-start(f32[288,256]{1,0:T(8,128)} %constant.19.clone.table_ref) | copy-start | bytes 884740
  14.7 58.7 %copy-start = (bf16[1024,256]{1,0:T(8,128)(2,1)S(1)}, bf16[1024,256]{1,0:T(8,128)(2,1)}, u32[]{:S(2)}) copy-start(bf16[1024,256]{1,0:T(8,128)(2,1)} %constant.20.clone.first_ref) | copy-start | bytes 1572868
  14.7 58.7 %copy-start.4 = (f32[2,256,128]{2,1,0:T(8,128)S(1)}, f32[2,256,128]{2,1,0:T(8,128)}, u32[]{:S(2)}) copy-start(f32[2,256,128]{2,1,0:T(8,128)} %constant.21.clone.turn_ref) | copy-start | bytes 786436
  14.7 58.7 %copy-start.5 = (bf16[256,256]{1,0:T(8,128)(2,1)S(1)}, bf16[256,256]{1,0:T(8,128)(2,1)}, u32[]{:S(2)}) copy-start(bf16[256,256]{1,0:T(8,128)(2,1)} %constant.22.clone.last_ref) | copy-start | bytes 393220
  73.4 18.2 %copy-start.1 = (bf16[192,1024]{1,0:T(8,128)(2,1)S(1)}, bf16[192,1024]{1,0:T(8,128)(2,1)}, u32[]{:S(2)}) copy-start(bf16[192,1024]{1,0:T(8,128)(2,1)} %constant.23.clone.table_ref) | copy-start | bytes 1179652

commit v3 on v2

--- a/solution.py
+++ b/solution.py
@@ -16,7 +16,6 @@
 GY = 8
 NN = (((1,), (0,)), ((), ()))
 NT = (((1,), (1,)), ((), ()))
-TN = (((0,), (0,)), ((), ()))
 
 
 def np_split(table):
@@ -48,7 +47,7 @@
     b = np.arange(inner)[None, :]
     turn = angles(b * (2 * l + 1), 2 * NY)
     turn = np.concatenate([np.cos(turn), np.sin(turn)], 1)
-    sub, j = np.meshgrid(np.arange(16), np.arange(GY), indexing="ij")
+    j, sub = np.meshgrid(np.arange(GY), np.arange(16), indexing="ij")
     m = np.where(sub < 8, 8 * j + sub, 127 - 8 * j - (sub - 8)).reshape(-1, 1)
     last = angles(2 * b * m, inner)
     last = np.concatenate([np.cos(last), -np.sin(last)], 1)
@@ -64,7 +63,8 @@
 def x_tables():
     outer, inner = 256, 16
     l = np.concatenate([np.arange(0, outer, 2), np.arange(1, outer, 2)])[:, None]
-    phase = angles(np.arange(outer)[None, :] * (2 * l + 1), 2 * outer)
+    a = np.arange(outer).reshape(64, 2, 2).transpose(1, 0, 2).reshape(1, outer)
+    phase = angles(a * (2 * l + 1), 2 * outer)
     first = np.concatenate(np_split(np.concatenate([np.cos(phase), np.sin(phase)], 0)), 0)
     lanes = np.arange(128)[None, :]
     b = lanes // 8
@@ -86,50 +86,37 @@
     for ly in range(4):
         column = np.where(sub < 8, 32 * sub + 4 * octet + ly, 32 * (sub - 8) + 31 - 4 * octet - ly)
         table[src, ly, column] = 1
-    return np.concatenate([table.reshape(GX, 1024)] * 3, 0).astype(jnp.bfloat16)
-
-
-def scale_kernel(ids, length_in, amplitude_in, mean_in, x_in, o_ref, mean_ref, length, amplitude, mean, x_ref, sems):
-    moves = [
-        pltpu.make_async_copy(source, target, sems.at[k])
-        for k, (source, target) in enumerate(
-            [(x_in, x_ref), (length_in, length), (amplitude_in, amplitude), (mean_in, mean)]
-        )
-    ]
-    for move in moves:
-        move.start()
+    return table.reshape(GX, 1024).astype(jnp.bfloat16)
+
+
+def y_kernel(length, amplitude, mean, x_ref, table_ref, o_ref, mean_ref, s_ref, w_ref):
+    gx, gy = lax.axis_index("gx"), lax.axis_index("gy")
+    plane, half = gy // 4, gy % 2
     norming = math.sqrt(2.0 * math.pi) / math.sqrt(NX * NY)
-    row = ids[0] * 64 + lax.broadcasted_iota(jnp.int32, (64, 128), 0)
+    row = gx * 64 + gy // 2 % 2 * 32 + lax.broadcasted_iota(jnp.int32, (32, 128), 0)
     row_wave = row.astype(F32) * (1.0 / NX)
     row_wave = row_wave * row_wave
     row_weight = jnp.where(row == 0, math.sqrt(1.0 / NX), math.sqrt(2.0 / NX))
-    for move in moves:
-        move.wait()
-    for c in range(4):
-        col = ids[1] * 512 + c * 128 + lax.broadcasted_iota(jnp.int32, (64, 128), 1)
+    lane = lax.broadcasted_iota(jnp.int32, (32, 128), 1)
+    reach = math.pi * length[plane]
+    factor = amplitude[plane] * length[plane] * norming
+    for a in range(16):
+        col = (a // 4 * 8 + half * 4 + a % 4) * 128 + lane
         col_wave = col.astype(F32) * (1.0 / NY)
         weight = row_weight * jnp.where(col == 0, math.sqrt(1.0 / NY), math.sqrt(2.0 / NY))
-        radius = row_wave + col_wave * col_wave
-        for p in range(2):
-            reach = math.pi * length[p]
-            root = lax.rsqrt(1.0 + reach * reach * radius)
-            factor = amplitude[p] * length[p] * norming
-            spectrum = factor * (root * jnp.sqrt(root))
-            scaled = x_ref[0, p, :, c * 128:(c + 1) * 128] * spectrum * weight
-            o_ref[:, c, p] = scaled.reshape(4, 16, 128)
+        root = lax.rsqrt(1.0 + reach * reach * (row_wave + col_wave * col_wave))
+        spectrum = factor * (root * jnp.sqrt(root))
+        block = x_ref[a // 4, :, a % 4 * 128:a % 4 * 128 + 128]
+        s_ref[32 * a:32 * a + 32, :] = block * spectrum * weight
     for p in range(2):
         mean_ref[p] = jnp.full((8, 128), mean[p], F32)
-
-
-def y_kernel(ids, x_ref, table_ref, o_ref, w_ref):
-    half = ids[1] % 2
     first = table_ref[pl.ds(pl.multiple_of(half * 64, 64), 64), :128].astype(BF16)[:, :48]
     turn_c, turn_s = table_ref[128:160, :128], table_ref[128:160, 128:]
     last = jnp.concatenate(split(table_ref[160:288, :]), 0)
     for group in range(4):
         pieces = []
         for line in range(8 * group, 8 * group + 8):
-            high, low = split(x_ref[pl.ds(line, 16, stride=32), :])
+            high, low = split(s_ref[pl.ds(line, 16, stride=32), :])
             pieces.append(jnp.concatenate([high, low, high], 0))
         part = mul(first, jnp.concatenate(pieces, 1), NN)
         for k in range(8):
@@ -141,15 +128,18 @@
         high, low = split(w_ref[octet].reshape(256, 256))
         both = mul(last, high, NT)
         out = both[:128] + both[128:] + mul(last[:128], low, NT)
-        for p in range(2):
-            o_ref[pl.ds(octet * 256 + p, 128, stride=2), :] = out[:, p * 128:(p + 1) * 128]
+        for j in range(GY):
+            for side in range(2):
+                block = out[16 * j:16 * j + 16, 128 * side:128 * side + 128]
+                o_ref[pl.ds(128 * j + 32 * octet + side, 16, stride=2), :] = block
 
 
 def x_kernel(mean_ref, x_ref, first_ref, turn_ref, last_ref, o_ref):
     total = jnp.zeros((64, 128), F32)
     turn_c, turn_s = turn_ref[0], turn_ref[1]
     for p in range(2):
-        values = x_ref[pl.ds(p, 256, stride=4), :] + x_ref[pl.ds(p + 2, 256, stride=4), :]
+        halves = [x_ref[k:k + 128] + x_ref[k + 128:k + 256] for k in (512 * p, 512 * p + 256)]
+        values = jnp.concatenate(halves, 0)
         both = mul(first_ref[...], jnp.concatenate(split(values), 1), NN)
         part = both[:512, :128] + (both[:512, 128:] + both[512:, :128])
         part_c, part_s = part[:256], part[256:]
@@ -174,21 +164,23 @@
         o_ref[:, 7 - q, :] = row[8:]
 
 
-def place_kernel(ids, x_ref, table_ref, o_ref):
-    values = x_ref[...]
-    high, rest = values.astype(BF16), values - values.astype(BF16).astype(F32)
-    middle, low = split(rest)
-    spread = mul(jnp.concatenate([high, middle, low], 0), table_ref[...], TN)
-    out = spread[:32, :256]
-    for ly in range(1, 4):
-        out = out + spread[32 * ly:32 * ly + 32, 256 * ly:256 * ly + 256]
-    back = ids[0] // 4 % 2
+def place_kernel(x_ref, table_ref, o_ref):
+    values = x_ref[...].T
+    high = values.astype(BF16)
+    middle, low = split(values - high.astype(F32))
+    out = jnp.zeros((32, 256), F32)
+    for ly in range(4):
+        rows = slice(32 * ly, 32 * ly + 32)
+        parts = jnp.concatenate([high[rows], middle[rows], low[rows]], 0)
+        spread = mul(parts, table_ref[:, 256 * ly:256 * ly + 256], NN)
+        out = out + (spread[:32] + (spread[32:64] + spread[64:]))
+    back = lax.axis_index("gx") // 4 % 2
     for r in range(32):
         o_ref[pl.ds(jnp.where(back == 1, 31 - r, r), 1), :] = out[r:r + 1]
 
 
 def call(kernel, shapes, places, scratch=()):
-    spaces = {"s": pltpu.SMEM, "v": pltpu.VMEM, "h": pltpu.HBM}
+    spaces = {"s": pltpu.SMEM, "v": pltpu.VMEM}
     outs = [jax.ShapeDtypeStruct(shape, F32) for shape in shapes]
     result = pl.pallas_call(
         kernel,
@@ -202,25 +194,21 @@
 
 
 def body(normals, plane_length, plane_amplitude, plane_mean):
-    ids = jnp.stack([lax.axis_index("gx"), lax.axis_index("gy")]).astype(jnp.int32)
-    scratch = [pltpu.SMEM((2,), F32)] * 3 + [pltpu.VMEM((1, 2, 64, 512), F32), pltpu.SemaphoreType.DMA((4,))]
-    scaled, mean = call(scale_kernel, [(4, 4, 2, 16, 128), (2, 8, 128)], "shhhh", scratch)(
-        ids, plane_length, plane_amplitude, plane_mean, normals
-    )
     sides = [[2 * y + h for y in range(4)] for h in range(2)]
     lines = lax.all_to_all(
-        scaled.reshape(4, 128, 128), "gy", 0, 0, tiled=True, axis_index_groups=sides
-    )
-    (rows,) = call(y_kernel, [(1024, 128)], "svv", [pltpu.VMEM((4, 32, 8, 256), F32)])(
-        ids, lines.reshape(512, 128), y_tables()
-    )
-    rows = lax.all_to_all(rows.reshape(512, 2, 128), ("gx", "gy"), 0, 0, tiled=True)
+        normals.reshape(4, 32, 512), "gy", 0, 0, tiled=True, axis_index_groups=sides
+    )
+    scratch = [pltpu.VMEM((512, 128), F32), pltpu.VMEM((4, 32, 8, 256), F32)]
+    rows, mean = call(y_kernel, [(1024, 128), (2, 8, 128)], "sssvv", scratch)(
+        plane_length, plane_amplitude, plane_mean, lines, y_tables()
+    )
+    rows = lax.all_to_all(rows.reshape(512, 2, 128), ("gy", "gx"), 0, 0, tiled=True)
     first, turn, last = x_tables()
     (coarse,) = call(x_kernel, [(8, 8, 128)], "vvvvv")(
         mean, rows.reshape(1024, 128), first, turn, last
     )
     coarse = lax.all_to_all(coarse.reshape(64, 1, 128), "gx", 0, 0, tiled=True)
-    (out,) = call(place_kernel, [(32, 256)], "svv")(ids, coarse.reshape(64, 128), place_table())
+    (out,) = call(place_kernel, [(32, 256)], "vv")(coarse.reshape(64, 128), place_table())
     return out.reshape(1, 1, 32, 256)
 
 

time: 93.3 us -> 90 us (0.965)
  Pallas kernels: 5.27 us -> 3.64 us
  local copies, waits for them, and re-layouts: 1.59 us -> 0.04 us
    pallas_call x4 -> x3, Pallas kernels: 5.27 us -> 3.64 us  [call(): return lambda *operands: result(*operands)]
    unnamed x18 -> x16, local copies, waits for them, and re-layouts: 1.59 us -> 0.04 us
where the time goes in v3:
time: 90 us; the launch traced here: 89.8 us
  blocking collectives  86 us (96%)
  Pallas kernels  3.64 us (4%)
    all_to_all x1, blocking collectives, body(): lax.all_to_all(rows.reshape(512, 2, 128), ('gy', 'gx'), 0, 0, tiled=True)  58.6 us
    all_to_all x1, blocking collectives, body(): coarse = lax.all_to_all(coarse.reshape(64, 1, 128), 'gx', 0, 0, tiled=True)  16.7 us
    all_to_all x1, blocking collectives, body(): lax.all_to_all(normals.reshape(4, 32, 512), 'gy', 0, 0, tiled=True, axis_...  10.7 us
    pallas_call x3, Pallas kernels, call(): return lambda *operands: result(*operands)  3.64 us

profile of v3, /device:TPU:1, one launch (start us, length us, event | category | flops | bytes accessed | tf_op | source)
XLA Modules:
  0.0 89.8 jit_solution(7213533193537398084)
XLA Ops:
  0.0 0.0 copy-start.1
  0.0 0.0 copy-start.5
  0.0 0.0 copy-start.6
  0.0 0.0 copy-start.7
  0.0 10.7 %all_to_all.15.x_ref = f32[4,32,512]{2,1,0:T(8,128)S(1)} all-to-all(f32[4,32,512]{2,1,0:T(8,128)} %bitcast.12), channel_id=1, replica_groups={{0,2,4,6},{1,3,5,7},{8,10,12,14},{9,11,13,15},{16,18,20,22},{17,19,21,2..., dimensions={0} | all-to-all | bytes 524288 | tf_op jit(solution)/shard_map/all_to_all | solution.py:198
  10.7 0.0 copy-done.1
  10.7 0.0 copy-done.5
  10.7 0.0 copy-done.6
  10.7 0.0 copy-done.7
  10.7 1.5 %shard_map.91 = (f32[1024,128]{1,0:T(8,128)S(1)}, f32[2,8,128]{2,1,0:T(8,128)S(1)}) custom-call(f32[2]{0:T(128)S(1)} %copy-done.5, f32[2]{0:T(128)S(1)} %copy-done.6, f32[2]{0:T(128)S(1)} %copy-done.7, f32[4,32,512]{2,1,0:T(8,128)S(1)} %all_to_all.15.x_ref, f32[288,256]{1,0:T(8,128)S(1)} %copy-done.1), custom_call_target="tpu_custom_call" | custom-call | tf_op jit(solution)/shard_map/pallas_call | solution.py:193
  12.2 0.0 copy-start
  12.2 0.0 copy-start.2
  12.2 0.0 copy-start.3
  12.2 58.6 %all_to_all.16 = f32[512,2,128]{2,1,0:T(2,128)S(1)} all-to-all(f32[512,2,128]{2,1,0:T(2,128)S(1)} %bitcast.9), channel_id=1, replica_groups=mesh['gx'=64,'gy'=8] {'gy','gx'}, dimensions={0} | all-to-all | bytes 1048576 | tf_op jit(solution)/shard_map/all_to_all | solution.py:205
  70.9 0.0 copy-done
  70.9 0.0 copy-done.2
  70.9 0.0 copy-done.3
  70.9 0.0 copy-start.4
  70.9 1.3 %shard_map.92 = f32[8,8,128]{2,1,0:T(8,128)S(1)} custom-call(f32[2,8,128]{2,1,0:T(8,128)S(1)} %get-tuple-element.7.mean_ref, f32[1024,128]{1,0:T(8,128)S(1)} %bitcast.8, bf16[1024,256]{1,0:T(8,128)(2,1)S(1)} %copy-done, f32[2,256,128]{2,1,0:T(8,128)S(1)} %copy-done.2, bf16[256,256]{1,0:T(8,128)(2,1)S(1)} %copy-done.3), custom_call_target="tpu_custom_call" | custom-call | tf_op jit(solution)/shard_map/pallas_call | solution.py:193
  72.2 16.7 %all_to_all.17 = f32[64,1,128]{2,1,0:T(1,128)S(1)} all-to-all(f32[64,1,128]{2,1,0:T(1,128)S(1)} %bitcast.10), channel_id=1, replica_groups=mesh['gx'=64,'gy'=8] {'gx'}, dimensions={0} | all-to-all | bytes 65536 | tf_op jit(solution)/shard_map/all_to_all | solution.py:210
  88.9 0.0 copy-done.4
  88.9 0.9 %shard_map.93 = f32[32,256]{1,0:T(8,128)} custom-call(f32[64,128]{1,0:T(8,128)S(1)} %bitcast.11, bf16[64,1024]{1,0:T(8,128)(2,1)S(1)} %copy-done.4), custom_call_target="tpu_custom_call" | custom-call | tf_op jit(solution)/shard_map/pallas_call | solution.py:193
Async XLA Ops:
  0.0 10.7 %copy-start.1 = (f32[288,256]{1,0:T(8,128)S(1)}, f32[288,256]{1,0:T(8,128)}, u32[]{:S(2)}) copy-start(f32[288,256]{1,0:T(8,128)} %constant.10.clone.table_ref) | copy-start | bytes 884740
  0.0 10.7 %copy-start.5 = (f32[2]{0:T(128)S(1)}, f32[2]{0:T(128)}, u32[]{:S(2)}) copy-start(f32[2]{0:T(128)} %length.1) | copy-start | bytes 28
  0.0 10.7 %copy-start.6 = (f32[2]{0:T(128)S(1)}, f32[2]{0:T(128)}, u32[]{:S(2)}) copy-start(f32[2]{0:T(128)} %amplitude.1) | copy-start | bytes 28
  0.0 10.7 %copy-start.7 = (f32[2]{0:T(128)S(1)}, f32[2]{0:T(128)}, u32[]{:S(2)}) copy-start(f32[2]{0:T(128)} %mean.1) | copy-start | bytes 28
  12.2 58.7 %copy-start = (bf16[1024,256]{1,0:T(8,128)(2,1)S(1)}, bf16[1024,256]{1,0:T(8,128)(2,1)}, u32[]{:S(2)}) copy-start(bf16[1024,256]{1,0:T(8,128)(2,1)} %constant.11.clone.first_ref) | copy-start | bytes 1572868
  12.2 58.7 %copy-start.2 = (f32[2,256,128]{2,1,0:T(8,128)S(1)}, f32[2,256,128]{2,1,0:T(8,128)}, u32[]{:S(2)}) copy-start(f32[2,256,128]{2,1,0:T(8,128)} %constant.12.clone.turn_ref) | copy-start | bytes 786436
  12.2 58.6 %copy-start.3 = (bf16[256,256]{1,0:T(8,128)(2,1)S(1)}, bf16[256,256]{1,0:T(8,128)(2,1)}, u32[]{:S(2)}) copy-start(bf16[256,256]{1,0:T(8,128)(2,1)} %constant.13.clone.last_ref) | copy-start | bytes 393220
  70.9 18.0 %copy-start.4 = (bf16[64,1024]{1,0:T(8,128)(2,1)S(1)}, bf16[64,1024]{1,0:T(8,128)(2,1)}, u32[]{:S(2)}) copy-start(bf16[64,1024]{1,0:T(8,128)(2,1)} %constant.14.clone.table_ref) | copy-start | bytes 393220

commit v4 on v3

--- a/solution.py
+++ b/solution.py
@@ -93,21 +93,23 @@
     gx, gy = lax.axis_index("gx"), lax.axis_index("gy")
     plane, half = gy // 4, gy % 2
     norming = math.sqrt(2.0 * math.pi) / math.sqrt(NX * NY)
+    reach = math.pi * length[plane]
+    factor = amplitude[plane] * length[plane] * norming * math.sqrt(2.0 / NY)
     row = gx * 64 + gy // 2 % 2 * 32 + lax.broadcasted_iota(jnp.int32, (32, 128), 0)
-    row_wave = row.astype(F32) * (1.0 / NX)
-    row_wave = row_wave * row_wave
-    row_weight = jnp.where(row == 0, math.sqrt(1.0 / NX), math.sqrt(2.0 / NX))
-    lane = lax.broadcasted_iota(jnp.int32, (32, 128), 1)
-    reach = math.pi * length[plane]
-    factor = amplitude[plane] * length[plane] * norming
+    row_part = reach * (row.astype(F32) * (1.0 / NX))
+    row_part = 1.0 + row_part * row_part
+    scale = factor * jnp.where(row == 0, math.sqrt(1.0 / NX), math.sqrt(2.0 / NX))
+    lane = lax.broadcasted_iota(jnp.int32, (8, 128), 1)
     for a in range(16):
         col = (a // 4 * 8 + half * 4 + a % 4) * 128 + lane
-        col_wave = col.astype(F32) * (1.0 / NY)
-        weight = row_weight * jnp.where(col == 0, math.sqrt(1.0 / NY), math.sqrt(2.0 / NY))
-        root = lax.rsqrt(1.0 + reach * reach * (row_wave + col_wave * col_wave))
-        spectrum = factor * (root * jnp.sqrt(root))
-        block = x_ref[a // 4, :, a % 4 * 128:a % 4 * 128 + 128]
-        s_ref[32 * a:32 * a + 32, :] = block * spectrum * weight
+        col_part = reach * (col.astype(F32) * (1.0 / NY))
+        col_part = col_part * col_part
+        root = lax.rsqrt(row_part + jnp.concatenate([col_part] * 4, 0))
+        spectrum = root * root * lax.rsqrt(root) * scale
+        if a == 0:
+            first_col = jnp.where(col == 0, math.sqrt(0.5), 1.0).astype(F32)
+            spectrum = spectrum * jnp.concatenate([first_col] * 4, 0)
+        s_ref[32 * a:32 * a + 32, :] = x_ref[a // 4, :, a % 4 * 128:a % 4 * 128 + 128] * spectrum
     for p in range(2):
         mean_ref[p] = jnp.full((8, 128), mean[p], F32)
     first = table_ref[pl.ds(pl.multiple_of(half * 64, 64), 64), :128].astype(BF16)[:, :48]
@@ -137,12 +139,15 @@
 def x_kernel(mean_ref, x_ref, first_ref, turn_ref, last_ref, o_ref):
     total = jnp.zeros((64, 128), F32)
     turn_c, turn_s = turn_ref[0], turn_ref[1]
+    planes = []
     for p in range(2):
         halves = [x_ref[k:k + 128] + x_ref[k + 128:k + 256] for k in (512 * p, 512 * p + 256)]
-        values = jnp.concatenate(halves, 0)
-        both = mul(first_ref[...], jnp.concatenate(split(values), 1), NN)
-        part = both[:512, :128] + (both[:512, 128:] + both[512:, :128])
-        part_c, part_s = part[:256], part[256:]
+        planes.append(jnp.concatenate(halves, 0))
+    high, low = split(jnp.concatenate(planes, 1))
+    both = mul(first_ref[...], high, NN)
+    part = both[:512] + (both[512:] + mul(first_ref[:512, :], low, NN))
+    for p in range(2):
+        part_c, part_s = part[:256, 128 * p:128 * p + 128], part[256:, 128 * p:128 * p + 128]
         turned = jnp.concatenate(
             [part_c * turn_c - part_s * turn_s, part_c * turn_s + part_s * turn_c], 1
         )

time: 90 us -> 89.6 us (level)
  no operation moved by 1% of the time
where the time goes in v4:
time: 89.6 us; the launch traced here: 89.4 us
  blocking collectives  86 us (96%)
  Pallas kernels  3.23 us (4%)
    all_to_all x1, blocking collectives, body(): lax.all_to_all(rows.reshape(512, 2, 128), ('gy', 'gx'), 0, 0, tiled=True)  58.6 us
    all_to_all x1, blocking collectives, body(): coarse = lax.all_to_all(coarse.reshape(64, 1, 128), 'gx', 0, 0, tiled=True)  16.7 us
    all_to_all x1, blocking collectives, body(): lax.all_to_all(normals.reshape(4, 32, 512), 'gy', 0, 0, tiled=True, axis_...  10.7 us
    pallas_call x3, Pallas kernels, call(): return lambda *operands: result(*operands)  3.23 us

profile of v4, /device:TPU:1, one launch (start us, length us, event | category | flops | bytes accessed | tf_op | source)
XLA Modules:
  0.0 89.4 jit_solution(15722576762262830473)
XLA Ops:
  0.0 0.0 copy-start.1
  0.0 0.0 copy-start.5
  0.0 0.0 copy-start.6
  0.0 0.0 copy-start.7
  0.0 10.7 %all_to_all.15.x_ref = f32[4,32,512]{2,1,0:T(8,128)S(1)} all-to-all(f32[4,32,512]{2,1,0:T(8,128)} %bitcast.12), channel_id=1, replica_groups={{0,2,4,6},{1,3,5,7},{8,10,12,14},{9,11,13,15},{16,18,20,22},{17,19,21,2..., dimensions={0} | all-to-all | bytes 524288 | tf_op jit(solution)/shard_map/all_to_all | solution.py:203
  10.7 0.0 copy-done.1
  10.7 0.0 copy-done.5
  10.7 0.0 copy-done.6
  10.7 0.0 copy-done.7
  10.7 1.3 %shard_map.91 = (f32[1024,128]{1,0:T(8,128)S(1)}, f32[2,8,128]{2,1,0:T(8,128)S(1)}) custom-call(f32[2]{0:T(128)S(1)} %copy-done.5, f32[2]{0:T(128)S(1)} %copy-done.6, f32[2]{0:T(128)S(1)} %copy-done.7, f32[4,32,512]{2,1,0:T(8,128)S(1)} %all_to_all.15.x_ref, f32[288,256]{1,0:T(8,128)S(1)} %copy-done.1), custom_call_target="tpu_custom_call" | custom-call | tf_op jit(solution)/shard_map/pallas_call | solution.py:198
  12.1 0.0 copy-start
  12.1 0.0 copy-start.2
  12.1 0.0 copy-start.3
  12.1 58.6 %all_to_all.16 = f32[512,2,128]{2,1,0:T(2,128)S(1)} all-to-all(f32[512,2,128]{2,1,0:T(2,128)S(1)} %bitcast.9), channel_id=1, replica_groups=mesh['gx'=64,'gy'=8] {'gy','gx'}, dimensions={0} | all-to-all | bytes 1048576 | tf_op jit(solution)/shard_map/all_to_all | solution.py:210
  70.7 0.0 copy-done
  70.7 0.0 copy-done.2
  70.7 0.0 copy-done.3
  70.8 0.0 copy-start.4
  70.8 1.0 %shard_map.92 = f32[8,8,128]{2,1,0:T(8,128)S(1)} custom-call(f32[2,8,128]{2,1,0:T(8,128)S(1)} %get-tuple-element.7.mean_ref, f32[1024,128]{1,0:T(8,128)S(1)} %bitcast.8, bf16[1024,256]{1,0:T(8,128)(2,1)S(1)} %copy-done, f32[2,256,128]{2,1,0:T(8,128)S(1)} %copy-done.2, bf16[256,256]{1,0:T(8,128)(2,1)S(1)} %copy-done.3), custom_call_target="tpu_custom_call" | custom-call | tf_op jit(solution)/shard_map/pallas_call | solution.py:198
  71.8 16.7 %all_to_all.17 = f32[64,1,128]{2,1,0:T(1,128)S(1)} all-to-all(f32[64,1,128]{2,1,0:T(1,128)S(1)} %bitcast.10), channel_id=1, replica_groups=mesh['gx'=64,'gy'=8] {'gx'}, dimensions={0} | all-to-all | bytes 65536 | tf_op jit(solution)/shard_map/all_to_all | solution.py:215
  88.5 0.0 copy-done.4
  88.5 0.9 %shard_map.93 = f32[32,256]{1,0:T(8,128)} custom-call(f32[64,128]{1,0:T(8,128)S(1)} %bitcast.11, bf16[64,1024]{1,0:T(8,128)(2,1)S(1)} %copy-done.4), custom_call_target="tpu_custom_call" | custom-call | tf_op jit(solution)/shard_map/pallas_call | solution.py:198
Async XLA Ops:
  0.0 10.7 %copy-start.1 = (f32[288,256]{1,0:T(8,128)S(1)}, f32[288,256]{1,0:T(8,128)}, u32[]{:S(2)}) copy-start(f32[288,256]{1,0:T(8,128)} %constant.10.clone.table_ref) | copy-start | bytes 884740
  0.0 10.7 %copy-start.5 = (f32[2]{0:T(128)S(1)}, f32[2]{0:T(128)}, u32[]{:S(2)}) copy-start(f32[2]{0:T(128)} %length.1) | copy-start | bytes 28
  0.0 10.7 %copy-start.6 = (f32[2]{0:T(128)S(1)}, f32[2]{0:T(128)}, u32[]{:S(2)}) copy-start(f32[2]{0:T(128)} %amplitude.1) | copy-start | bytes 28
  0.0 10.7 %copy-start.7 = (f32[2]{0:T(128)S(1)}, f32[2]{0:T(128)}, u32[]{:S(2)}) copy-start(f32[2]{0:T(128)} %mean.1) | copy-start | bytes 28
  12.1 58.7 %copy-start = (bf16[1024,256]{1,0:T(8,128)(2,1)S(1)}, bf16[1024,256]{1,0:T(8,128)(2,1)}, u32[]{:S(2)}) copy-start(bf16[1024,256]{1,0:T(8,128)(2,1)} %constant.11.clone.first_ref) | copy-start | bytes 1572868
  12.1 58.7 %copy-start.2 = (f32[2,256,128]{2,1,0:T(8,128)S(1)}, f32[2,256,128]{2,1,0:T(8,128)}, u32[]{:S(2)}) copy-start(f32[2,256,128]{2,1,0:T(8,128)} %constant.12.clone.turn_ref) | copy-start | bytes 786436
  12.1 58.6 %copy-start.3 = (bf16[256,256]{1,0:T(8,128)(2,1)S(1)}, bf16[256,256]{1,0:T(8,128)(2,1)}, u32[]{:S(2)}) copy-start(bf16[256,256]{1,0:T(8,128)(2,1)} %constant.13.clone.last_ref) | copy-start | bytes 393220
  70.8 17.7 %copy-start.4 = (bf16[64,1024]{1,0:T(8,128)(2,1)S(1)}, bf16[64,1024]{1,0:T(8,128)(2,1)}, u32[]{:S(2)}) copy-start(bf16[64,1024]{1,0:T(8,128)(2,1)} %constant.14.clone.table_ref) | copy-start | bytes 393220

commit v5 on v4

--- a/solution.py
+++ b/solution.py
@@ -93,8 +93,12 @@
     gx, gy = lax.axis_index("gx"), lax.axis_index("gy")
     plane, half = gy // 4, gy % 2
     norming = math.sqrt(2.0 * math.pi) / math.sqrt(NX * NY)
-    reach = math.pi * length[plane]
-    factor = amplitude[plane] * length[plane] * norming * math.sqrt(2.0 / NY)
+    own_length, own_amplitude = [
+        jnp.where(plane == 0, values[:, 0:1], values[:, 1:2])
+        for values in (length[...].reshape(1, 2), amplitude[...].reshape(1, 2))
+    ]
+    reach = math.pi * own_length
+    factor = own_amplitude * own_length * (norming * math.sqrt(2.0 / NY))
     row = gx * 64 + gy // 2 % 2 * 32 + lax.broadcasted_iota(jnp.int32, (32, 128), 0)
     row_part = reach * (row.astype(F32) * (1.0 / NX))
     row_part = 1.0 + row_part * row_part
@@ -110,8 +114,9 @@
             first_col = jnp.where(col == 0, math.sqrt(0.5), 1.0).astype(F32)
             spectrum = spectrum * jnp.concatenate([first_col] * 4, 0)
         s_ref[32 * a:32 * a + 32, :] = x_ref[a // 4, :, a % 4 * 128:a % 4 * 128 + 128] * spectrum
+    values = mean[...].reshape(1, 2)
     for p in range(2):
-        mean_ref[p] = jnp.full((8, 128), mean[p], F32)
+        mean_ref[p] = jnp.broadcast_to(values[:, p:p + 1], (8, 128))
     first = table_ref[pl.ds(pl.multiple_of(half * 64, 64), 64), :128].astype(BF16)[:, :48]
     turn_c, turn_s = table_ref[128:160, :128], table_ref[128:160, 128:]
     last = jnp.concatenate(split(table_ref[160:288, :]), 0)
@@ -184,13 +189,12 @@
         o_ref[pl.ds(jnp.where(back == 1, 31 - r, r), 1), :] = out[r:r + 1]
 
 
-def call(kernel, shapes, places, scratch=()):
-    spaces = {"s": pltpu.SMEM, "v": pltpu.VMEM}
+def call(kernel, shapes, inputs, scratch=()):
     outs = [jax.ShapeDtypeStruct(shape, F32) for shape in shapes]
     result = pl.pallas_call(
         kernel,
         out_shape=outs,
-        in_specs=[pl.BlockSpec(memory_space=spaces[place]) for place in places],
+        in_specs=[pl.BlockSpec(memory_space=pltpu.VMEM)] * inputs,
         out_specs=[pl.BlockSpec(memory_space=pltpu.VMEM)] * len(outs),
         scratch_shapes=list(scratch),
         compiler_params=pltpu.CompilerParams(vmem_limit_bytes=32 * 1024 * 1024),
@@ -204,16 +208,16 @@
         normals.reshape(4, 32, 512), "gy", 0, 0, tiled=True, axis_index_groups=sides
     )
     scratch = [pltpu.VMEM((512, 128), F32), pltpu.VMEM((4, 32, 8, 256), F32)]
-    rows, mean = call(y_kernel, [(1024, 128), (2, 8, 128)], "sssvv", scratch)(
+    rows, mean = call(y_kernel, [(1024, 128), (2, 8, 128)], 5, scratch)(
         plane_length, plane_amplitude, plane_mean, lines, y_tables()
     )
     rows = lax.all_to_all(rows.reshape(512, 2, 128), ("gy", "gx"), 0, 0, tiled=True)
     first, turn, last = x_tables()
-    (coarse,) = call(x_kernel, [(8, 8, 128)], "vvvvv")(
+    (coarse,) = call(x_kernel, [(8, 8, 128)], 5)(
         mean, rows.reshape(1024, 128), first, turn, last
     )
     coarse = lax.all_to_all(coarse.reshape(64, 1, 128), "gx", 0, 0, tiled=True)
-    (out,) = call(place_kernel, [(32, 256)], "vv")(coarse.reshape(64, 128), place_table())
+    (out,) = call(place_kernel, [(32, 256)], 2)(coarse.reshape(64, 128), place_table())
     return out.reshape(1, 1, 32, 256)
 
 

time: 89.6 us -> 89.2 us (level)
  no operation moved by 1% of the time
where the time goes in v5:
time: 89.2 us; the launch traced here: 89 us
  blocking collectives  86 us (96%)
  Pallas kernels  2.82 us (3%)
    all_to_all x1, blocking collectives, body(): lax.all_to_all(rows.reshape(512, 2, 128), ('gy', 'gx'), 0, 0, tiled=True)  58.6 us
    all_to_all x1, blocking collectives, body(): coarse = lax.all_to_all(coarse.reshape(64, 1, 128), 'gx', 0, 0, tiled=True)  16.7 us
    all_to_all x1, blocking collectives, body(): lax.all_to_all(normals.reshape(4, 32, 512), 'gy', 0, 0, tiled=True, axis_...  10.7 us
    pallas_call x3, Pallas kernels, call(): return lambda *operands: result(*operands)  2.82 us

profile of v5, /device:TPU:1, one launch (start us, length us, event | category | flops | bytes accessed | tf_op | source)
XLA Modules:
  0.0 89.0 jit_solution(14022499240190222562)
XLA Ops:
  0.0 0.0 copy-start.1
  0.0 0.0 copy-start.5
  0.0 0.0 copy-start.6
  0.0 0.0 copy-start.7
  0.0 10.7 %all_to_all.15.x_ref = f32[4,32,512]{2,1,0:T(8,128)S(1)} all-to-all(f32[4,32,512]{2,1,0:T(8,128)} %bitcast.12), channel_id=1, replica_groups={{0,2,4,6},{1,3,5,7},{8,10,12,14},{9,11,13,15},{16,18,20,22},{17,19,21,2..., dimensions={0} | all-to-all | bytes 524288 | tf_op jit(solution)/shard_map/all_to_all | solution.py:207
  10.7 0.0 copy-done.1
  10.7 0.0 copy-done.5
  10.7 0.0 copy-done.6
  10.7 0.0 copy-done.7
  10.7 0.9 %shard_map.91 = (f32[1024,128]{1,0:T(8,128)S(1)}, f32[2,8,128]{2,1,0:T(8,128)S(1)}) custom-call(f32[2]{0:T(128)S(1)} %copy-done.5, f32[2]{0:T(128)S(1)} %copy-done.6, f32[2]{0:T(128)S(1)} %copy-done.7, f32[4,32,512]{2,1,0:T(8,128)S(1)} %all_to_all.15.x_ref, f32[288,256]{1,0:T(8,128)S(1)} %copy-done.1), custom_call_target="tpu_custom_call" | custom-call | tf_op jit(solution)/shard_map/pallas_call | solution.py:202
  11.7 0.0 copy-start
  11.7 0.0 copy-start.2
  11.7 0.0 copy-start.3
  11.7 58.6 %all_to_all.16 = f32[512,2,128]{2,1,0:T(2,128)S(1)} all-to-all(f32[512,2,128]{2,1,0:T(2,128)S(1)} %bitcast.9), channel_id=1, replica_groups=mesh['gx'=64,'gy'=8] {'gy','gx'}, dimensions={0} | all-to-all | bytes 1048576 | tf_op jit(solution)/shard_map/all_to_all | solution.py:214
  70.3 0.0 copy-done
  70.3 0.0 copy-done.2
  70.3 0.0 copy-done.3
  70.3 0.0 copy-start.4
  70.4 1.0 %shard_map.92 = f32[8,8,128]{2,1,0:T(8,128)S(1)} custom-call(f32[2,8,128]{2,1,0:T(8,128)S(1)} %get-tuple-element.7.mean_ref, f32[1024,128]{1,0:T(8,128)S(1)} %bitcast.8, bf16[1024,256]{1,0:T(8,128)(2,1)S(1)} %copy-done, f32[2,256,128]{2,1,0:T(8,128)S(1)} %copy-done.2, bf16[256,256]{1,0:T(8,128)(2,1)S(1)} %copy-done.3), custom_call_target="tpu_custom_call" | custom-call | tf_op jit(solution)/shard_map/pallas_call | solution.py:202
  71.4 16.7 %all_to_all.17 = f32[64,1,128]{2,1,0:T(1,128)S(1)} all-to-all(f32[64,1,128]{2,1,0:T(1,128)S(1)} %bitcast.10), channel_id=1, replica_groups=mesh['gx'=64,'gy'=8] {'gx'}, dimensions={0} | all-to-all | bytes 65536 | tf_op jit(solution)/shard_map/all_to_all | solution.py:219
  88.0 0.0 copy-done.4
  88.1 0.9 %shard_map.93 = f32[32,256]{1,0:T(8,128)} custom-call(f32[64,128]{1,0:T(8,128)S(1)} %bitcast.11, bf16[64,1024]{1,0:T(8,128)(2,1)S(1)} %copy-done.4), custom_call_target="tpu_custom_call" | custom-call | tf_op jit(solution)/shard_map/pallas_call | solution.py:202
Async XLA Ops:
  0.0 10.7 %copy-start.1 = (f32[288,256]{1,0:T(8,128)S(1)}, f32[288,256]{1,0:T(8,128)}, u32[]{:S(2)}) copy-start(f32[288,256]{1,0:T(8,128)} %constant.10.clone.table_ref) | copy-start | bytes 884740
  0.0 10.7 %copy-start.5 = (f32[2]{0:T(128)S(1)}, f32[2]{0:T(128)}, u32[]{:S(2)}) copy-start(f32[2]{0:T(128)} %length.1) | copy-start | bytes 28
  0.0 10.7 %copy-start.6 = (f32[2]{0:T(128)S(1)}, f32[2]{0:T(128)}, u32[]{:S(2)}) copy-start(f32[2]{0:T(128)} %amplitude.1) | copy-start | bytes 28
  0.0 10.7 %copy-start.7 = (f32[2]{0:T(128)S(1)}, f32[2]{0:T(128)}, u32[]{:S(2)}) copy-start(f32[2]{0:T(128)} %mean.1) | copy-start | bytes 28
  11.7 58.7 %copy-start = (bf16[1024,256]{1,0:T(8,128)(2,1)S(1)}, bf16[1024,256]{1,0:T(8,128)(2,1)}, u32[]{:S(2)}) copy-start(bf16[1024,256]{1,0:T(8,128)(2,1)} %constant.11.clone.first_ref) | copy-start | bytes 1572868
  11.7 58.7 %copy-start.2 = (f32[2,256,128]{2,1,0:T(8,128)S(1)}, f32[2,256,128]{2,1,0:T(8,128)}, u32[]{:S(2)}) copy-start(f32[2,256,128]{2,1,0:T(8,128)} %constant.12.clone.turn_ref) | copy-start | bytes 786436
  11.7 58.6 %copy-start.3 = (bf16[256,256]{1,0:T(8,128)(2,1)S(1)}, bf16[256,256]{1,0:T(8,128)(2,1)}, u32[]{:S(2)}) copy-start(bf16[256,256]{1,0:T(8,128)(2,1)} %constant.13.clone.last_ref) | copy-start | bytes 393220
  70.3 17.7 %copy-start.4 = (bf16[64,1024]{1,0:T(8,128)(2,1)S(1)}, bf16[64,1024]{1,0:T(8,128)(2,1)}, u32[]{:S(2)}) copy-start(bf16[64,1024]{1,0:T(8,128)(2,1)} %constant.14.clone.table_ref) | copy-start | bytes 393220

commit v6 on v5

--- a/solution.py
+++ b/solution.py
@@ -89,7 +89,7 @@
     return table.reshape(GX, 1024).astype(jnp.bfloat16)
 
 
-def y_kernel(length, amplitude, mean, x_ref, table_ref, o_ref, mean_ref, s_ref, w_ref):
+def y_kernel(length, amplitude, mean, x_ref, table_ref, o_ref, mean_ref, s_ref, w_ref, sent_ref):
     gx, gy = lax.axis_index("gx"), lax.axis_index("gy")
     plane, half = gy // 4, gy % 2
     norming = math.sqrt(2.0 * math.pi) / math.sqrt(NX * NY)
@@ -138,7 +138,8 @@
         for j in range(GY):
             for side in range(2):
                 block = out[16 * j:16 * j + 16, 128 * side:128 * side + 128]
-                o_ref[pl.ds(128 * j + 32 * octet + side, 16, stride=2), :] = block
+                sent_ref[pl.ds(128 * j + 32 * octet + side, 16, stride=2), :] = block
+    o_ref[...] = sent_ref[:1024, :]
 
 
 def x_kernel(mean_ref, x_ref, first_ref, turn_ref, last_ref, o_ref):
@@ -207,7 +208,9 @@
     lines = lax.all_to_all(
         normals.reshape(4, 32, 512), "gy", 0, 0, tiled=True, axis_index_groups=sides
     )
-    scratch = [pltpu.VMEM((512, 128), F32), pltpu.VMEM((4, 32, 8, 256), F32)]
+    scratch = [
+        pltpu.VMEM(shape, F32) for shape in ((544, 128), (4, 32, 8, 256), (1032, 128))
+    ]
     rows, mean = call(y_kernel, [(1024, 128), (2, 8, 128)], 5, scratch)(
         plane_length, plane_amplitude, plane_mean, lines, y_tables()
     )

time: 89.2 us -> 89.2 us (level)
  no operation moved by 1% of the time
where the time goes in v6:
time: 89.2 us; the launch traced here: 89 us
  blocking collectives  86 us (96%)
  Pallas kernels  2.84 us (3%)
    all_to_all x1, blocking collectives, body(): lax.all_to_all(rows.reshape(512, 2, 128), ('gy', 'gx'), 0, 0, tiled=True)  58.6 us
    all_to_all x1, blocking collectives, body(): coarse = lax.all_to_all(coarse.reshape(64, 1, 128), 'gx', 0, 0, tiled=True)  16.7 us
    all_to_all x1, blocking collectives, body(): lax.all_to_all(normals.reshape(4, 32, 512), 'gy', 0, 0, tiled=True, axis_...  10.7 us
    pallas_call x3, Pallas kernels, call(): return lambda *operands: result(*operands)  2.84 us

profile of v6, /device:TPU:1, one launch (start us, length us, event | category | flops | bytes accessed | tf_op | source)
XLA Modules:
  0.0 89.0 jit_solution(10278561868186030776)
XLA Ops:
  0.0 0.0 copy-start.1
  0.0 0.0 copy-start.5
  0.0 0.0 copy-start.6
  0.0 0.0 copy-start.7
  0.0 10.7 %all_to_all.15.x_ref = f32[4,32,512]{2,1,0:T(8,128)S(1)} all-to-all(f32[4,32,512]{2,1,0:T(8,128)} %bitcast.12), channel_id=1, replica_groups={{0,2,4,6},{1,3,5,7},{8,10,12,14},{9,11,13,15},{16,18,20,22},{17,19,21,2..., dimensions={0} | all-to-all | bytes 524288 | tf_op jit(solution)/shard_map/all_to_all | solution.py:208
  10.7 0.0 copy-done.1
  10.7 0.0 copy-done.5
  10.7 0.0 copy-done.6
  10.7 0.0 copy-done.7
  10.7 1.0 %shard_map.91 = (f32[1024,128]{1,0:T(8,128)S(1)}, f32[2,8,128]{2,1,0:T(8,128)S(1)}) custom-call(f32[2]{0:T(128)S(1)} %copy-done.5, f32[2]{0:T(128)S(1)} %copy-done.6, f32[2]{0:T(128)S(1)} %copy-done.7, f32[4,32,512]{2,1,0:T(8,128)S(1)} %all_to_all.15.x_ref, f32[288,256]{1,0:T(8,128)S(1)} %copy-done.1), custom_call_target="tpu_custom_call" | custom-call | tf_op jit(solution)/shard_map/pallas_call | solution.py:203
  11.7 0.0 copy-start
  11.7 0.0 copy-start.2
  11.7 0.0 copy-start.3
  11.7 58.6 %all_to_all.16 = f32[512,2,128]{2,1,0:T(2,128)S(1)} all-to-all(f32[512,2,128]{2,1,0:T(2,128)S(1)} %bitcast.9), channel_id=1, replica_groups=mesh['gx'=64,'gy'=8] {'gy','gx'}, dimensions={0} | all-to-all | bytes 1048576 | tf_op jit(solution)/shard_map/all_to_all | solution.py:217
  70.4 0.0 copy-done
  70.4 0.0 copy-done.2
  70.4 0.0 copy-done.3
  70.4 0.0 copy-start.4
  70.4 1.0 %shard_map.92 = f32[8,8,128]{2,1,0:T(8,128)S(1)} custom-call(f32[2,8,128]{2,1,0:T(8,128)S(1)} %get-tuple-element.7.mean_ref, f32[1024,128]{1,0:T(8,128)S(1)} %bitcast.8, bf16[1024,256]{1,0:T(8,128)(2,1)S(1)} %copy-done, f32[2,256,128]{2,1,0:T(8,128)S(1)} %copy-done.2, bf16[256,256]{1,0:T(8,128)(2,1)S(1)} %copy-done.3), custom_call_target="tpu_custom_call" | custom-call | tf_op jit(solution)/shard_map/pallas_call | solution.py:203
  71.4 16.7 %all_to_all.17 = f32[64,1,128]{2,1,0:T(1,128)S(1)} all-to-all(f32[64,1,128]{2,1,0:T(1,128)S(1)} %bitcast.10), channel_id=1, replica_groups=mesh['gx'=64,'gy'=8] {'gx'}, dimensions={0} | all-to-all | bytes 65536 | tf_op jit(solution)/shard_map/all_to_all | solution.py:222
  88.1 0.0 copy-done.4
  88.1 0.9 %shard_map.93 = f32[32,256]{1,0:T(8,128)} custom-call(f32[64,128]{1,0:T(8,128)S(1)} %bitcast.11, bf16[64,1024]{1,0:T(8,128)(2,1)S(1)} %copy-done.4), custom_call_target="tpu_custom_call" | custom-call | tf_op jit(solution)/shard_map/pallas_call | solution.py:203
Async XLA Ops:
  0.0 10.7 %copy-start.1 = (f32[288,256]{1,0:T(8,128)S(1)}, f32[288,256]{1,0:T(8,128)}, u32[]{:S(2)}) copy-start(f32[288,256]{1,0:T(8,128)} %constant.10.clone.table_ref) | copy-start | bytes 884740
  0.0 10.7 %copy-start.5 = (f32[2]{0:T(128)S(1)}, f32[2]{0:T(128)}, u32[]{:S(2)}) copy-start(f32[2]{0:T(128)} %length.1) | copy-start | bytes 28
  0.0 10.7 %copy-start.6 = (f32[2]{0:T(128)S(1)}, f32[2]{0:T(128)}, u32[]{:S(2)}) copy-start(f32[2]{0:T(128)} %amplitude.1) | copy-start | bytes 28
  0.0 10.7 %copy-start.7 = (f32[2]{0:T(128)S(1)}, f32[2]{0:T(128)}, u32[]{:S(2)}) copy-start(f32[2]{0:T(128)} %mean.1) | copy-start | bytes 28
  11.7 58.7 %copy-start = (bf16[1024,256]{1,0:T(8,128)(2,1)S(1)}, bf16[1024,256]{1,0:T(8,128)(2,1)}, u32[]{:S(2)}) copy-start(bf16[1024,256]{1,0:T(8,128)(2,1)} %constant.11.clone.first_ref) | copy-start | bytes 1572868
  11.7 58.7 %copy-start.2 = (f32[2,256,128]{2,1,0:T(8,128)S(1)}, f32[2,256,128]{2,1,0:T(8,128)}, u32[]{:S(2)}) copy-start(f32[2,256,128]{2,1,0:T(8,128)} %constant.12.clone.turn_ref) | copy-start | bytes 786436
  11.7 58.6 %copy-start.3 = (bf16[256,256]{1,0:T(8,128)(2,1)S(1)}, bf16[256,256]{1,0:T(8,128)(2,1)}, u32[]{:S(2)}) copy-start(bf16[256,256]{1,0:T(8,128)(2,1)} %constant.13.clone.last_ref) | copy-start | bytes 393220
  70.4 17.7 %copy-start.4 = (bf16[64,1024]{1,0:T(8,128)(2,1)S(1)}, bf16[64,1024]{1,0:T(8,128)(2,1)}, u32[]{:S(2)}) copy-start(bf16[64,1024]{1,0:T(8,128)(2,1)} %constant.14.clone.table_ref) | copy-start | bytes 393220
